TPU v7x, 256 devices: a whole 4x4x8 slice. The times are simulated.
256 devices in a mesh: dp: 32 (over x, z), proto: 8 (over y, core).
Axes of the slice: x: 4, y: 4, z: 8, core: 2. Of those that a mesh axis runs over, the one named last changes fastest.
Arguments:
- teacher_feat: bfloat16 [16384, 256], P('dp'), may hold values from -16 to 16
- student_feat: bfloat16 [16384, 256], P('dp'), may hold values from -16 to 16
- teacher_protos: bfloat16 [65536, 256], P('proto'), may hold values from -16 to 16
- student_protos: bfloat16 [65536, 256], P('proto'), may hold values from -16 to 16
Outputs:
- row_loss: float32 [16384], P('dp')
- feature_grad: bfloat16 [16384, 256], P('dp')
- proto_grad: bfloat16 [65536, 256], P(('proto', 'dp'))
All inputs are finite; a program needn't handle non-finite values.
Results may differ from a plain program's by a relative error of at most 0.0069.
Values may be sent and summed in bfloat16 or wider, within the bound.
No kernel may reach another device: no remote copies, remote signals or barrier semaphores. Data moves between devices by JAX's collectives and lax.ppermute only.
A program may use at most 128 MiB of HBM per device.

v0:
```python
import jax
import jax.numpy as jnp
from jax import lax
from jax.sharding import PartitionSpec as P

ITERS = 3


teacher_temp = 0.07
student_temp = 0.1


def unit_rows(x):
    xf = x.astype(jnp.float32)
    return (xf * lax.rsqrt(jnp.sum(xf * xf, axis=1, keepdims=True) + 1e-06)).astype(jnp.bfloat16)


def by_rows(left, right):
    return lax.dot_general(
        left, right, (((1,), (1,)), ((), ())), preferred_element_type=jnp.float32
    )


def by_cols(left, right):
    return lax.dot_general(
        left, right, (((0,), (0,)), ((), ())), preferred_element_type=jnp.float32
    )


def local(teacher_feat, student_feat, teacher_protos, student_protos):
    t_unit = unit_rows(teacher_feat)
    s_unit = unit_rows(student_feat)
    t_dirs = unit_rows(teacher_protos)
    s_dirs = unit_rows(student_protos)
    rows_local = t_unit.shape[0]
    protos_local = t_dirs.shape[0]
    data_count = lax.axis_size("dp")
    batch_total = rows_local * data_count
    proto_total = protos_local * lax.axis_size("proto")
    expo = jnp.exp(by_rows(t_unit, t_dirs) / teacher_temp)
    row_scale = jnp.ones((rows_local,), jnp.float32)
    col_scale = jnp.ones((protos_local,), jnp.float32)
    row_total = jnp.ones((rows_local,), jnp.float32)
    for step in range(ITERS):
        local_col = jnp.dot(
            row_scale, expo, precision=lax.Precision.HIGHEST, preferred_element_type=jnp.float32
        )
        col_whole = lax.psum(local_col, "dp")
        col_scale = 1.0 / (proto_total * col_whole)
        local_row = jnp.dot(
            expo, col_scale, precision=lax.Precision.HIGHEST, preferred_element_type=jnp.float32
        )
        row_total = lax.psum(local_row, "proto")
        row_scale = 1.0 / (batch_total * row_total)
    targets = expo * col_scale[None, :] / row_total[:, None]
    logits = by_rows(s_unit, s_dirs) / student_temp
    expl = jnp.exp(logits)
    totals, cross = lax.psum((jnp.sum(expl, axis=1), jnp.sum(targets * logits, axis=1)), "proto")
    row_loss = jnp.log(totals) - cross
    factor = proto_total / (batch_total * student_temp)
    dlog = ((expl / totals[:, None] - targets) * factor).astype(jnp.bfloat16)
    feature_terms = jnp.dot(dlog, s_dirs, preferred_element_type=jnp.float32)
    feature_grad = lax.psum(feature_terms, "proto").astype(jnp.bfloat16)
    proto_grad = lax.psum_scatter(by_cols(dlog, s_unit), "dp", scatter_dimension=0, tiled=True)
    return (row_loss, feature_grad, proto_grad.astype(jnp.bfloat16))


def solution(mesh):
    placed = (P("dp", None), P("dp", None), P("proto", None), P("proto", None))
    return jax.shard_map(
        local,
        mesh=mesh,
        in_specs=placed,
        out_specs=(P("dp"), P("dp", None), P(("proto", "dp"), None)),
        check_vma=False,
    )
```

profile of v0, /device:TPU:1, one launch (start us, length us, event | category | flops | bytes accessed | tf_op | source)
XLA Modules:
  0.0 843.0 jit_solution(2574433222485155690)
XLA Ops:
  7.2 0.0 reduce-scatter.2.cloned.1.call-start
  7.2 1.1 fusion.12
  8.3 1.1 fusion.10
  9.4 3.3 fusion.2
  12.8 3.3 fusion
  16.2 5.1 multiply_exponential_fusion
  21.3 0.0 copy-start
  21.3 5.7 copy-done
  27.0 7.9 fusion.19
  35.0 119.2 %psum.64 = f32[8192]{0:T(1024)S(1)} all-reduce(f32[8192]{0:T(1024)S(1)} %bitcast.29), channel_id=1, replica_groups=mesh['dp'=32,'proto'=8] {'dp'}, use_global_device_ids=true, to_apply=%region_6.0 | all-reduce | flops 8192 | bytes 65536 | tf_op jit(solution)/shard_map/psum | solution.py:48
  154.2 17.6 %fusion.22 = f32[1,512]{1,0:T(1,128)S(1)} fusion(f32[512,8192]{1,0:T(8,128)} %copy-done, f32[8192,1]{0,1:T(1,128)S(1)} %bitcast.25), kind=kOutput, calls=%fused_computation.39 | convolution fusion | flops 50331648 | bytes 16812032 | tf_op jit(solution)/shard_map/dot_general | solution.py:50
  171.8 40.5 %psum.65 = f32[512]{0:T(512)S(1)} all-reduce(f32[512]{0:T(512)S(1)} %bitcast.30), channel_id=1, replica_groups=mesh['dp'=32,'proto'=8] {'proto'}, use_global_device_ids=true, to_apply=%region_7.0 | all-reduce | flops 512 | bytes 4096 | tf_op jit(solution)/shard_map/psum | solution.py:53
  212.3 11.5 %fusion.23 = f32[1,8192]{1,0:T(1,128)S(1)} fusion(f32[512,1]{0,1:T(1,128)S(1)} %bitcast.33, f32[512,8192]{1,0:T(8,128)} %copy-done), kind=kOutput, calls=%fused_computation.40 | convolution fusion | flops 50331648 | bytes 16812032 | tf_op jit(solution)/shard_map/dot_general | solution.py:45
  223.7 110.8 %psum.66 = f32[8192]{0:T(1024)S(1)} all-reduce(f32[8192]{0:T(1024)S(1)} %bitcast.26), channel_id=1, replica_groups=mesh['dp'=32,'proto'=8] {'dp'}, use_global_device_ids=true, to_apply=%region_8.0 | all-reduce | flops 8192 | bytes 65536 | tf_op jit(solution)/shard_map/psum | solution.py:48
  334.5 17.6 %fusion.24 = f32[1,512]{1,0:T(1,128)S(1)} fusion(f32[512,8192]{1,0:T(8,128)} %copy-done, f32[8192,1]{0,1:T(1,128)S(1)} %bitcast.27), kind=kOutput, calls=%fused_computation.41 | convolution fusion | flops 50331648 | bytes 16812032 | tf_op jit(solution)/shard_map/dot_general | solution.py:50
  352.1 39.3 %psum.67 = f32[512]{0:T(512)S(1)} all-reduce(f32[512]{0:T(512)S(1)} %bitcast.31), channel_id=1, replica_groups=mesh['dp'=32,'proto'=8] {'proto'}, use_global_device_ids=true, to_apply=%region_9.0 | all-reduce | flops 512 | bytes 4096 | tf_op jit(solution)/shard_map/psum | solution.py:53
  391.5 11.5 %fusion.25 = f32[1,8192]{1,0:T(1,128)S(1)} fusion(f32[512,1]{0,1:T(1,128)S(1)} %bitcast.34, f32[512,8192]{1,0:T(8,128)} %copy-done), kind=kOutput, calls=%fused_computation.42 | convolution fusion | flops 50331648 | bytes 16812032 | tf_op jit(solution)/shard_map/dot_general | solution.py:45
  402.9 0.0 copy-start.2
  402.9 110.2 %psum.68 = f32[8192]{0:T(1024)S(1)} all-reduce(f32[8192]{0:T(1024)S(1)} %bitcast.28), channel_id=1, replica_groups=mesh['dp'=32,'proto'=8] {'dp'}, use_global_device_ids=true, to_apply=%region_10.0 | all-reduce | flops 8192 | bytes 65536 | tf_op jit(solution)/shard_map/psum | solution.py:48
  513.1 17.6 %fusion.26 = f32[1,512]{1,0:T(1,128)S(1)} fusion(f32[512,8192]{1,0:T(8,128)} %copy-done, f32[8192,1]{0,1:T(1,128)S(1)} %bitcast.24), kind=kOutput, calls=%fused_computation.43 | convolution fusion | flops 50331648 | bytes 16812032 | tf_op jit(solution)/shard_map/dot_general | solution.py:50
  530.8 40.2 %psum.69 = f32[512]{0:T(512)S(1)} all-reduce(f32[512]{0:T(512)S(1)} %bitcast.32), channel_id=1, replica_groups=mesh['dp'=32,'proto'=8] {'proto'}, use_global_device_ids=true, to_apply=%region_11.0 | all-reduce | flops 512 | bytes 4096 | tf_op jit(solution)/shard_map/psum | solution.py:53
  571.0 0.0 copy-done.2
  571.0 13.7 %exponential_reduce_fusion = (f32[512]{0:T(512)S(1)}, f32[512]{0:T(512)S(1)}, f32[512,8192]{1,0:T(8,128)}) fusion(f32[512]{0:T(512)S(1)} %psum.69, f32[512,8192]{1,0:T(8,128)} %copy-done, f32[8192]{0:T(1024)S(1)} %multiply_divide_fusion.1, bf16[8192,256]{1,0:T(8,128)(2,1)} %param.7, f32[8192]{0:T(1024)S(1)} %add_rsqrt_fusion.1, ...), kind=kOutput, calls=%fused_computation.4 | convolution fusion | flops 2179333120 | bytes 38084608 | tf_op jit(solution)/shard_map/dot_general | solution.py:19
  584.7 12.6 %psum.63 = f32[512]{0:T(512)S(1)} all-reduce(f32[512]{0:T(512)S(1)} %get-tuple-element.3), channel_id=1, replica_groups=mesh['dp'=32,'proto'=8] {'proto'}, use_global_device_ids=true, to_apply=%region_3.0 | all-reduce | flops 512 | bytes 4096 | tf_op jit(solution)/shard_map/psum | solution.py:58
  597.3 12.1 %multiply_convert_fusion = bf16[512,8192]{1,0:T(8,128)(2,1)S(1)} fusion(f32[512,8192]{1,0:T(8,128)} %get-tuple-element.7, f32[512]{0:T(512)S(1)} %psum.63, f32[512]{0:T(512)S(1)} %psum.69, f32[512,8192]{1,0:T(8,128)} %copy-done, f32[8192]{0:T(1024)S(1)} %multiply_divide_fusion.1), kind=kLoop, calls=%fused_computation | loop fusion | flops 29360128 | bytes 41979904 | tf_op jit(solution)/shard_map/convert_element_type | solution.py:61
  609.4 0.0 copy-start.1
  609.4 3.2 copy-done.1
  612.6 5.7 fusion.16
  618.3 0.0 reduce-scatter.2.cloned.1.call-update
  618.3 7.3 fusion.6
  625.6 27.8 %all-reduce.2 = (f32[512]{0:T(512)S(1)}, bf16[512,256]{1,0:T(8,128)(2,1)}) all-reduce(f32[512]{0:T(512)S(1)} %get-tuple-element.4, f32[512,256]{1,0:T(8,128)S(1)} %fusion.6), channel_id=1, replica_groups=mesh['dp'=32,'proto'=8] {'proto'}, use_global_device_ids=true, to_apply=%region_13.0 | all-reduce | flops 131584 | bytes 790528 | tf_op jit(solution)/shard_map/psum | solution.py:58
  653.4 0.6 log_subtract_fusion
  654.0 180.3 %reduce-scatter.2.cloned.1.call-done = f32[256,256]{1,0:T(8,128)} async-done(((f32[8192,256]{1,0:T(8,128)}), f32[256,256]{1,0:T(8,128)}) %reduce-scatter.2.cloned.1.call-update) | async-done | bytes 262160 | tf_op jit(solution)/shard_map/reduce_scatter | solution.py:64
  834.3 1.6 convert_element_type.43
  (9 shorter events, 0.1 us)
Async XLA Ops:
  7.2 827.1 %reduce-scatter.2.cloned.1.call-start = ((), (), s32[]{:S(2)}) async-start(), calls=%async_computation.1 | async-start | bytes 8650752 | tf_op jit(solution)/shard_map/reduce_scatter | solution.py:64
  21.3 5.7 copy-start
  402.9 168.1 %copy-start.2 = (bf16[512,256]{1,0:T(8,128)(2,1)S(1)}, bf16[512,256]{1,0:T(8,128)(2,1)}, u32[]{:S(2)}) copy-start(bf16[512,256]{1,0:T(8,128)(2,1)} %param.5) | copy-start | bytes 786436
  609.4 3.2 copy-start.1
Sparse Core Ops, SparseCore 0:
  618.5 215.7 reduce-scatter.1
where the time goes:
time: 849 us; the launch traced here: 843 us
  blocking collectives  501 us (59%)
  waiting for transfers between devices  180 us (21%)
  matrix products  115 us (14%)
  other arithmetic  23.3 us (3%)
  between operations  14.4 us (2%)
  local copies, waits for them, and re-layouts  8.92 us (1%)
    psum x3, blocking collectives, local(): col_whole = lax.psum(local_col, 'dp')  340 us
    reduce_scatter x1, waiting for transfers between devices, local(): lax.psum_scatter(by_cols(dlog, s_unit), 'dp', scatter_dimension=0, tiled=...  180 us
    psum x3, blocking collectives, local(): row_total = lax.psum(local_row, 'proto')  120 us
    dot_general x3, matrix products, local(): jnp.dot(expo, col_scale, precision=lax.Precision.HIGHEST, preferred_eleme...  52.9 us
    psum x2, blocking collectives, local(): lax.psum((jnp.sum(expl, axis=1), jnp.sum(targets * logits, axis=1)), 'pro...  40.5 us
    dot_general x3, matrix products, local(): jnp.dot(row_scale, expo, precision=lax.Precision.HIGHEST, preferred_eleme...  30.8 us
    dot_general x2, matrix products, by_rows(): lax.dot_general(left, right, (((1,), (1,)), ((), ())), preferred_element_...  18.8 us
  transfers between devices with their start and end apart: 1, of which 1 were waited for; matrix products, arithmetic and copies ran while one was open for 1% of the time, Pallas kernels for 0%

commit v1 on v0

v1 whole, which is shorter than its diff:
```python
import functools
import math

import jax
import jax.numpy as jnp
from jax import lax
from jax.experimental import pallas as pl
from jax.experimental.pallas import tpu as pltpu
from jax.sharding import Mesh, PartitionSpec as P

f32 = jnp.float32
bf16 = jnp.bfloat16

NX, NZ, NY, NC = 4, 8, 4, 2
DIM = 256
PROTOS = 65536
BATCH = 16384
ROWS = BATCH // (NX * NZ)
COLS = PROTOS // (NY * NC)
BK = 1024
NB = COLS // BK
T_EXP2 = math.log2(math.e) / 0.07
S_EXP2 = math.log2(math.e) / 0.1
FACTOR = PROTOS / (BATCH * 0.1)
VMEM = 48 * 1024 * 1024

NT = (((1,), (1,)), ((), ()))
NN = (((1,), (0,)), ((), ()))


def dot(a, b, dims):
    return lax.dot_general(a, b, dims, preferred_element_type=f32)


def unit_rows(x):
    xf = x.astype(f32)
    return (xf * lax.rsqrt(jnp.sum(xf * xf, axis=1, keepdims=True) + 1e-06)).astype(bf16)


def split16(v):
    hi = v.astype(bf16).astype(f32)
    row = lax.broadcasted_iota(jnp.int32, (16, v.shape[1]), 0)
    return jnp.where(row == 0, hi, jnp.where(row == 1, v - hi, 0.0)).astype(bf16)


def lane_fold(m):
    acc = m[:, :128]
    for i in range(1, m.shape[1] // 128):
        acc = acc + m[:, i * 128 : (i + 1) * 128]
    return acc


def to_lanes(acc):
    return jnp.sum(acc.T, axis=0, keepdims=True)


def rows4(v):
    return jnp.concatenate([v[:, i * 128 : (i + 1) * 128] for i in range(4)], axis=0)


def lanes512(m):
    return jnp.concatenate([m[i : i + 1] for i in range(4)], axis=1)


def params():
    return pltpu.CompilerParams(vmem_limit_bytes=VMEM)


def call(kernel, grid, in_specs, out_specs, out_shape, scratch, flops, nbytes, name):
    return pl.pallas_call(
        kernel,
        grid=grid,
        in_specs=in_specs,
        out_specs=out_specs,
        out_shape=out_shape,
        scratch_shapes=scratch,
        compiler_params=params(),
        cost_estimate=pl.CostEstimate(flops=flops, bytes_accessed=nbytes, transcendentals=0),
        name=name,
    )


def whole(*shape):
    return pl.BlockSpec(shape, lambda j: (0,) * len(shape))


def teacher_kernel(feat, protos, unit_o, expo_o, cols_o, unit_s, cols_s):
    j = pl.program_id(0)

    @pl.when(j == 0)
    def _():
        u = unit_rows(feat[...])
        unit_s[...] = u
        unit_o[...] = u

    dirs = unit_rows(protos[...])
    expo = jnp.exp2(dot(unit_s[...], dirs, NT) * T_EXP2)
    expo_o[...] = expo.astype(bf16)
    cols_s[pl.ds(j, 1), :] = jnp.sum(expo, axis=0, keepdims=True)

    @pl.when(j == NB - 1)
    def _():
        cols_o[...] = jnp.broadcast_to(cols_s[...].astype(bf16)[None], cols_o.shape)


def teacher(feat, protos):
    return call(
        teacher_kernel,
        (NB,),
        [whole(ROWS, DIM), pl.BlockSpec((BK, DIM), lambda j: (j, 0))],
        [whole(ROWS, DIM), pl.BlockSpec((ROWS, BK), lambda j: (0, j)), whole(NX * NZ, NB, BK)],
        [
            jax.ShapeDtypeStruct((ROWS, DIM), bf16),
            jax.ShapeDtypeStruct((ROWS, COLS), bf16),
            jax.ShapeDtypeStruct((NX * NZ, NB, BK), bf16),
        ],
        [pltpu.VMEM((ROWS, DIM), bf16), pltpu.VMEM((NB, BK), f32)],
        2 * ROWS * COLS * DIM,
        ROWS * COLS * 2 + COLS * DIM * 2,
        "teacher",
    )(feat, protos)


def student_kernel(feat, protos, unit_o, dirs_o, tot_o, mix_o, unit_s, tot_s):
    j = pl.program_id(0)

    @pl.when(j == 0)
    def _():
        u = unit_rows(feat[...])
        unit_s[...] = u
        unit_o[...] = u
        tot_s[...] = jnp.zeros_like(tot_s)
        mix_o[...] = jnp.zeros_like(mix_o)

    dirs = unit_rows(protos[...])
    dirs_o[...] = dirs
    expl = jnp.exp2(dot(unit_s[...], dirs, NT) * S_EXP2)
    tot_s[...] += lane_fold(expl)
    mix_o[...] += dot(expl.astype(bf16), dirs, NN)

    @pl.when(j == NB - 1)
    def _():
        tot_o[...] = rows4(to_lanes(tot_s[...]))


def student(feat, protos):
    return call(
        student_kernel,
        (NB,),
        [whole(ROWS, DIM), pl.BlockSpec((BK, DIM), lambda j: (j, 0))],
        [whole(ROWS, DIM), pl.BlockSpec((BK, DIM), lambda j: (j, 0)), whole(4, 128), whole(ROWS, DIM)],
        [
            jax.ShapeDtypeStruct((ROWS, DIM), bf16),
            jax.ShapeDtypeStruct((COLS, DIM), bf16),
            jax.ShapeDtypeStruct((4, 128), f32),
            jax.ShapeDtypeStruct((ROWS, DIM), f32),
        ],
        [pltpu.VMEM((ROWS, DIM), bf16), pltpu.VMEM((ROWS, 128), f32)],
        4 * ROWS * COLS * DIM,
        COLS * DIM * 4,
        "student",
    )(feat, protos)


def col_scale(got):
    return 1.0 / (PROTOS * jnp.sum(got[...].astype(f32), axis=0))


def row_kernel(expo, got, rows_o, col_s, acc_s):
    j = pl.program_id(0)

    @pl.when(j == 0)
    def _():
        col_s[...] = col_scale(got)
        acc_s[...] = jnp.zeros_like(acc_s)

    acc_s[...] += dot(split16(col_s[pl.ds(j, 1), :]), expo[...], NT)

    @pl.when(j == NB - 1)
    def _():
        part = rows4(jnp.sum(acc_s[...], axis=0, keepdims=True))
        part = jnp.concatenate([part, jnp.zeros((4, 128), f32)], axis=0)
        rows_o[...] = jnp.broadcast_to(part[None], rows_o.shape)


def row_pass(expo, got):
    return call(
        row_kernel,
        (NB,),
        [pl.BlockSpec((ROWS, BK), lambda j: (0, j)), whole(NX * NZ, NB, BK)],
        whole(NY * NC, 8, 128),
        jax.ShapeDtypeStruct((NY * NC, 8, 128), f32),
        [pltpu.VMEM((NB, BK), f32), pltpu.VMEM((16, ROWS), f32)],
        2 * ROWS * COLS * 16,
        ROWS * COLS * 2,
        "row_pass",
    )(expo, got)


def col_kernel(expo, got, cols_o, lhs_s, cols_s):
    j = pl.program_id(0)

    @pl.when(j == 0)
    def _():
        total = lanes512(jnp.sum(got[...], axis=0)[:4])
        lhs_s[...] = split16(1.0 / (BATCH * total))

    part = dot(lhs_s[...], expo[...], NN)
    cols_s[pl.ds(j, 1), :] = jnp.sum(part, axis=0, keepdims=True)

    @pl.when(j == NB - 1)
    def _():
        cols_o[...] = jnp.broadcast_to(cols_s[...].astype(bf16)[None], cols_o.shape)


def col_pass(expo, got):
    return call(
        col_kernel,
        (NB,),
        [pl.BlockSpec((ROWS, BK), lambda j: (0, j)), whole(NY * NC, 8, 128)],
        whole(NX * NZ, NB, BK),
        jax.ShapeDtypeStruct((NX * NZ, NB, BK), bf16),
        [pltpu.VMEM((16, ROWS), bf16), pltpu.VMEM((NB, BK), f32)],
        2 * ROWS * COLS * 16,
        ROWS * COLS * 2,
        "col_pass",
    )(expo, got)


def last_kernel(expo, got, dirs, unit, tot, stat_o, mix_o, col_o, col_s, acc_s):
    j = pl.program_id(0)

    @pl.when(j == 0)
    def _():
        c = col_scale(got)
        col_s[...] = c
        col_o[...] = c
        acc_s[...] = jnp.zeros_like(acc_s)
        mix_o[...] = jnp.zeros_like(mix_o)

    w = expo[...].astype(f32) * col_s[pl.ds(j, 1), :]
    acc_s[...] += lane_fold(w)
    mix_o[...] += dot(w.astype(bf16), dirs[...], NN)

    @pl.when(j == NB - 1)
    def _():
        part = rows4(to_lanes(acc_s[...]))
        cross = rows4(to_lanes(lane_fold(mix_o[...] * unit[...].astype(f32)))) / 0.1
        stat = jnp.concatenate([part, cross, tot[...], jnp.zeros((4, 128), f32)], axis=0)
        stat_o[...] = jnp.broadcast_to(stat[None], stat_o.shape)


def last_pass(expo, got, dirs, unit, tot):
    n = NZ * NY * NC
    return call(
        last_kernel,
        (NB,),
        [
            pl.BlockSpec((ROWS, BK), lambda j: (0, j)),
            whole(NX * NZ, NB, BK),
            pl.BlockSpec((BK, DIM), lambda j: (j, 0)),
            whole(ROWS, DIM),
            whole(4, 128),
        ],
        [whole(n, 16, 128), whole(ROWS, DIM), whole(NB, BK)],
        [
            jax.ShapeDtypeStruct((n, 16, 128), f32),
            jax.ShapeDtypeStruct((ROWS, DIM), f32),
            jax.ShapeDtypeStruct((NB, BK), f32),
        ],
        [pltpu.VMEM((NB, BK), f32), pltpu.VMEM((ROWS, 128), f32)],
        2 * ROWS * COLS * DIM,
        ROWS * COLS * 2 + COLS * DIM * 2,
        "last_pass",
    )(expo, got, dirs, unit, tot)


def grad_kernel(pos, mine, other, stat, t_protos, s_dirs, col, out, dirs_s, col_s, acc_s, rows_s):
    k = pl.program_id(0)

    @pl.when(k == 0)
    def _():
        acc_s[...] = jnp.zeros_like(acc_s)
        for i in range(NX):
            dirs_s[i] = unit_rows(t_protos[i, 0])
            c = jnp.broadcast_to(col[i : i + 1, :], (128, DIM))
            col_s[i] = c.T

    core = pos[1]
    half = ROWS // NC
    rows_s[pl.ds(pl.multiple_of(core * half, half), half), :] = mine[0]
    rows_s[pl.ds(pl.multiple_of((1 - core) * half, half), half), :] = other[0]
    t_rows = rows_s[:, :DIM]
    s_rows = rows_s[:, DIM:]
    total = jnp.sum(stat[0], axis=0)
    t_scale = FACTOR / lanes512(total[0:4])
    s_scale = FACTOR / lanes512(total[8:12])
    for i in range(NX):
        expo = jnp.exp2(dot(dirs_s[i], t_rows, NT) * T_EXP2)
        expl = jnp.exp2(dot(s_dirs[i, 0], s_rows, NT) * S_EXP2)
        c = col_s[i]
        c = jnp.concatenate([c] * (ROWS // 128), axis=1)
        dlog = (expl * s_scale - expo * c * t_scale).astype(bf16)
        acc_s[i] += dot(dlog, s_rows, NN)

    @pl.when(k == NZ - 1)
    def _():
        out[...] = acc_s[...].astype(bf16)


def proto_part(pos, mine, other, stat, t_protos, s_dirs, col):
    half = ROWS // NC
    grid_spec = pltpu.PrefetchScalarGridSpec(
        num_scalar_prefetch=1,
        grid=(NZ,),
        in_specs=[
            pl.BlockSpec((1, half, 2 * DIM), lambda k, p: (p[2 + k], 0, 0)),
            pl.BlockSpec((1, half, 2 * DIM), lambda k, p: (p[2 + k], 0, 0)),
            pl.BlockSpec((1, NY * NC, 16, 128), lambda k, p: (p[2 + NZ + k], 0, 0, 0)),
            pl.BlockSpec((NX, 1, DIM, DIM), lambda k, p: (0, p[0], 0, 0)),
            pl.BlockSpec((NX, 1, DIM, DIM), lambda k, p: (0, p[0], 0, 0)),
            pl.BlockSpec((NX, DIM), lambda k, p: (0, 0)),
        ],
        out_specs=pl.BlockSpec((NX, DIM, DIM), lambda k, p: (0, 0, 0)),
        scratch_shapes=[
            pltpu.VMEM((NX, DIM, DIM), bf16),
            pltpu.VMEM((NX, DIM, 128), f32),
            pltpu.VMEM((NX, DIM, DIM), f32),
            pltpu.VMEM((ROWS, 2 * DIM), bf16),
        ],
    )
    return pl.pallas_call(
        grad_kernel,
        grid_spec=grid_spec,
        out_shape=jax.ShapeDtypeStruct((NX, DIM, DIM), bf16),
        compiler_params=params(),
        cost_estimate=pl.CostEstimate(
            flops=6 * ROWS * COLS * DIM, bytes_accessed=8 << 20, transcendentals=2 * ROWS * COLS
        ),
        name="proto_part",
    )(pos, mine, other, stat, t_protos, s_dirs, col)


def gather(a, axes):
    return lax.all_to_all(a, axes, 0, 0)


def swap_core(a):
    return lax.ppermute(a, "c", [(0, 1), (1, 0)])


def ring(a):
    up = down = a
    blocks = [a]
    for k in range(NZ // 2):
        up = lax.ppermute(up, "z", [(i, (i + 1) % NZ) for i in range(NZ)])
        blocks.append(up)
        if k < NZ // 2 - 1:
            down = lax.ppermute(down, "z", [(i, (i - 1) % NZ) for i in range(NZ)])
            blocks.append(down)
    return blocks


OFFSETS = (0, -1, 1, -2, 2, -3, 3, -4)


def local(teacher_feat, student_feat, teacher_protos, student_protos):
    z = lax.axis_index("z")
    core = lax.axis_index("c")
    half = ROWS // NC

    t_unit, expo, cols = teacher(teacher_feat, teacher_protos)
    s_unit, s_dirs, tot, s_mix = student(student_feat, student_protos)

    both = jnp.concatenate([t_unit, s_unit], axis=1)
    mine = jnp.stack(ring(lax.dynamic_slice_in_dim(both, core * half, half, 0)))
    other = swap_core(mine)

    for _ in range(2):
        rows = row_pass(expo, gather(cols, ("x", "z")))
        cols = col_pass(expo, gather(rows, ("y", "c")))
    stat, t_mix, col = last_pass(expo, gather(cols, ("x", "z")), s_dirs, s_unit, tot)
    stat = gather(stat, ("z", "y", "c")).reshape(NZ, NY * NC, 16, 128)

    order = (z + jnp.array(OFFSETS, jnp.int32)) % NZ
    pos = jnp.concatenate([jnp.stack([z, core]), jnp.arange(NZ, dtype=jnp.int32), order]).astype(jnp.int32)
    col_mine = lax.dynamic_index_in_dim(col.reshape(NX, NZ, DIM), z, 1, keepdims=False)
    part = proto_part(
        pos,
        mine,
        other,
        stat,
        teacher_protos.reshape(NX, NZ, DIM, DIM),
        s_dirs.reshape(NX, NZ, DIM, DIM),
        col_mine,
    )
    proto_grad = jnp.sum(gather(part, "x").astype(f32), axis=0).astype(bf16)

    own = jnp.sum(lax.dynamic_index_in_dim(stat, z, 0, keepdims=False), axis=0)
    row_total = own[0:4].reshape(ROWS)
    cross = own[4:8].reshape(ROWS) / row_total
    totals = own[8:12].reshape(ROWS)
    row_loss = jnp.log(totals) - cross

    terms = (s_mix / totals[:, None] - t_mix / row_total[:, None]) * FACTOR
    keep = lax.dynamic_slice_in_dim(terms, core * half, half, 0)
    give = lax.dynamic_slice_in_dim(terms, (1 - core) * half, half, 0)
    keep = (keep + swap_core(give.astype(bf16)).astype(f32)).astype(bf16)
    parts = gather(jnp.broadcast_to(keep[None], (NY, half, DIM)), "y")
    done = jnp.sum(parts.astype(f32), axis=0).astype(bf16)
    there = swap_core(done)
    feature_grad = jnp.where(
        core == 0, jnp.concatenate([done, there], 0), jnp.concatenate([there, done], 0)
    )
    return row_loss, feature_grad, proto_grad


def solution(mesh):
    fine = Mesh(mesh.devices.reshape(NX, NZ, NY, NC), ("x", "z", "y", "c"))
    rows, protos = P(("x", "z"), None), P(("y", "c"), None)
    return jax.shard_map(
        local,
        mesh=fine,
        in_specs=(rows, rows, protos, protos),
        out_specs=(P(("x", "z")), rows, P(("y", "c", "x", "z"), None)),
        check_vma=False,
    )
```

time: 849 us -> 223 us (0.26)
  blocking collectives: 501 us -> 26 us
  waiting for transfers between devices: 180 us -> 53.4 us
  matrix products: 115 us -> 0 us
  Pallas kernels: 0 us -> 70.2 us
  starting transfers between devices: 0.04 us -> 53.8 us
  other arithmetic: 23.3 us -> 3.31 us
  between operations: 14.4 us -> 0.79 us
    psum x8 -> x0, blocking collectives: 501 us -> none  [the longest x3 340 us: local(): col_whole = lax.psum(local_col, 'dp')]
    reduce_scatter x1 -> x0, waiting for transfers between devices: 180 us -> none  [local(): lax.psum_scatter(by_cols(dlog, s_unit), 'dp', scatter_dimension=0, tiled=...]
    dot_general x10 -> x0, matrix products: 115 us -> none  [the longest x3 52.9 us: local(): jnp.dot(expo, col_scale, precision=lax.Precision.HIGHEST, preferred_eleme...]
    pallas_call x0 -> x8, Pallas kernels: none -> 70.2 us  [the longest x2 15.6 us: row_pass(): call(row_kernel, (NB,), [pl.BlockSpec((ROWS, BK), lambda j: (0, j)), whol...]
    all_to_all x0 -> x7, starting transfers between devices: none -> 42.9 us  [gather(): return lax.all_to_all(a, axes, 0, 0)]
    all_to_all x0 -> x7, waiting for transfers between devices: none -> 33.1 us  [gather(): return lax.all_to_all(a, axes, 0, 0)]
    all_to_all x0 -> x1, blocking collectives: none -> 26 us  [gather(): return lax.all_to_all(a, axes, 0, 0)]
    ppermute x0 -> x10, waiting for transfers between devices: none -> 20.3 us  [the longest x3 13.8 us: ring(): down = lax.ppermute(down, 'z', [(i, (i - 1) % NZ) for i in range(NZ)])]
  transfers between devices with their start and end apart: 1 -> 17, of which waited for: 1 -> 8; matrix products, arithmetic and copies ran while one was open for 1% -> 4% of each run, Pallas kernels for 0% -> 22%
where the time goes in v1:
time: 223 us; the launch traced here: 221 us
  Pallas kernels  70.2 us (31%)
  starting transfers between devices  53.8 us (24%)
  waiting for transfers between devices  53.4 us (24%)
  blocking collectives  26 us (12%)
  local copies, waits for them, and re-layouts  13.3 us (6%)
  other arithmetic  3.31 us (1%)
    all_to_all x7, starting transfers between devices, gather(): return lax.all_to_all(a, axes, 0, 0)  42.9 us
    all_to_all x7, waiting for transfers between devices, gather(): return lax.all_to_all(a, axes, 0, 0)  33.1 us
    all_to_all x1, blocking collectives, gather(): return lax.all_to_all(a, axes, 0, 0)  26 us
    pallas_call x2, Pallas kernels, row_pass(): call(row_kernel, (NB,), [pl.BlockSpec((ROWS, BK), lambda j: (0, j)), whol...  15.6 us
    pallas_call x2, Pallas kernels, col_pass(): call(col_kernel, (NB,), [pl.BlockSpec((ROWS, BK), lambda j: (0, j)), whol...  14.9 us
    pallas_call x1, Pallas kernels, proto_part(): pl.pallas_call(grad_kernel, grid_spec=grid_spec, out_shape=jax.ShapeDtype...  14.6 us
    ppermute x3, waiting for transfers between devices, ring(): down = lax.ppermute(down, 'z', [(i, (i - 1) % NZ) for i in range(NZ)])  13.8 us
    unnamed x19, local copies, waits for them, and re-layouts  11.7 us
  transfers between devices with their start and end apart: 17, of which 8 were waited for; matrix products, arithmetic and copies ran while one was open for 4% of the time, Pallas kernels for 22%

profile of v1, /device:TPU:1, one launch (start us, length us, event | category | flops | bytes accessed | tf_op | source)
XLA Modules:
  0.0 220.7 jit_solution(7485178882744138300)
XLA Ops:
  0.6 2.2 copy-done.2
  2.8 0.9 copy-done.3
  3.8 7.3 %teacher.1 = (bf16[512,256]{1,0:T(8,128)(2,1)S(1)}, bf16[512,8192]{1,0:T(8,128)(2,1)}, bf16[32,8,1024]{2,1,0:T(8,128)(2,1)S(1)}) custom-call(bf16[512,256]{1,0:T(8,128)(2,1)S(1)} %copy-done.3, bf16[8192,256]{1,0:T(8,128)(2,1)S(1)} %copy-done.2), custom_call_target="tpu_custom_call" | custom-call | flops 2147483648 | bytes 12582912 | tf_op jit(solution)/shard_map/teacher/pallas_call | solution.py:107
  11.0 26.0 %all_to_all.40.got = bf16[32,8,1024]{2,1,0:T(8,128)(2,1)S(1)} all-to-all(bf16[32,8,1024]{2,1,0:T(8,128)(2,1)S(1)} %get-tuple-element.14), channel_id=1, replica_groups=mesh['x'=4,'z'=8,'y'=4,'c'=2] {'x','z'}, dimensions={0} | all-to-all | bytes 1048576 | tf_op jit(solution)/shard_map/all_to_all | solution.py:345
  37.0 7.8 %row_pass.2 = f32[8,8,128]{2,1,0:T(8,128)} custom-call(bf16[512,8192]{1,0:T(8,128)(2,1)} %get-tuple-element.13.expo, bf16[32,8,1024]{2,1,0:T(8,128)(2,1)S(1)} %all_to_all.40.got), custom_call_target="tpu_custom_call" | custom-call | flops 134217728 | bytes 8388608 | tf_op jit(solution)/shard_map/row_pass/pallas_call | solution.py:187
  44.8 8.0 %all-to-all-start.1 = ((f32[8,8,128]{2,1,0:T(8,128)}), f32[8,8,128]{2,1,0:T(8,128)S(1)}, u32[]{:S(2)}, u32[]{:S(2)}) async-start(f32[8,8,128]{2,1,0:T(8,128)} %row_pass.2), calls=%async_computation.1 | async-start | bytes 65536 | tf_op jit(solution)/shard_map/all_to_all | solution.py:345
  52.8 4.7 %all-to-all-done.1.got = f32[8,8,128]{2,1,0:T(8,128)S(1)} async-done(((f32[8,8,128]{2,1,0:T(8,128)}), f32[8,8,128]{2,1,0:T(8,128)S(1)}, u32[]{:S(2)}, u32[]{:S(2)}) %all-to-all-start.1) | async-done | bytes 32800 | tf_op jit(solution)/shard_map/all_to_all | solution.py:345
  57.5 7.5 %col_pass.2 = bf16[32,8,1024]{2,1,0:T(8,128)(2,1)} custom-call(bf16[512,8192]{1,0:T(8,128)(2,1)} %get-tuple-element.13.expo, f32[8,8,128]{2,1,0:T(8,128)S(1)} %all-to-all-done.1.got), custom_call_target="tpu_custom_call" | custom-call | flops 134217728 | bytes 8388608 | tf_op jit(solution)/shard_map/col_pass/pallas_call | solution.py:217
  65.0 5.3 %all-to-all-start.2 = ((bf16[32,8,1024]{2,1,0:T(8,128)(2,1)}), bf16[32,8,1024]{2,1,0:T(8,128)(2,1)S(1)}, u32[]{:S(2)}, u32[]{:S(2)}) async-start(bf16[32,8,1024]{2,1,0:T(8,128)(2,1)} %col_pass.2), calls=%async_computation.2 | async-start | bytes 1048576 | tf_op jit(solution)/shard_map/all_to_all | solution.py:345
  70.3 9.3 %student.1 = (bf16[512,256]{1,0:T(8,128)(2,1)S(1)}, bf16[8192,256]{1,0:T(8,128)(2,1)S(1)}, f32[4,128]{1,0:T(4,128)S(1)}, f32[512,256]{1,0:T(8,128)S(1)}) custom-call(bf16[512,256]{1,0:T(8,128)(2,1)S(1)} %copy-done.4, bf16[8192,256]{1,0:T(8,128)(2,1)} %protos.3), custom_call_target="tpu_custom_call" | custom-call | flops 4294967296 | bytes 8388608 | tf_op jit(solution)/shard_map/student/pallas_call | solution.py:147
  79.6 2.0 copy-done
  81.6 0.7 bitcast_dynamic-update-slice_fusion.7
  82.3 1.2 collective-permute-start.2
  83.6 1.4 collective-permute-start.3
  85.0 5.3 %collective-permute-done.2 = bf16[256,512]{1,0:T(8,128)(2,1)S(1)} collective-permute-done((bf16[256,512]{1,0:T(8,128)(2,1)S(1)}, bf16[256,512]{1,0:T(8,128)(2,1)S(1)}, u32[]{:S(2)}, u32[]{:S(2)}) %collective-permute-start.2) | collective-permute-done | bytes 262176 | tf_op jit(solution)/shard_map/ppermute | solution.py:356
  90.4 0.7 bitcast_dynamic-update-slice_fusion.6
  91.2 2.6 %collective-permute-start.5 = (bf16[256,512]{1,0:T(8,128)(2,1)S(1)}, bf16[256,512]{1,0:T(8,128)(2,1)S(1)}, u32[]{:S(2)}, u32[]{:S(2)}) collective-permute-start(bf16[256,512]{1,0:T(8,128)(2,1)S(1)} %collective-permute-done.3), channel_id=1, source_target_pairs={{0,56},{8,0},{16,8},{24,16},{32,24},{40,32},{48,40},{56,48},{1,57}... | collective-permute-start | bytes 786440 | tf_op jit(solution)/shard_map/ppermute | solution.py:359
  93.8 7.8 %row_pass.3 = f32[8,8,128]{2,1,0:T(8,128)} custom-call(bf16[512,8192]{1,0:T(8,128)(2,1)} %get-tuple-element.13.expo, bf16[32,8,1024]{2,1,0:T(8,128)(2,1)S(1)} %all-to-all-done.2.got), custom_call_target="tpu_custom_call" | custom-call | flops 134217728 | bytes 8388608 | tf_op jit(solution)/shard_map/row_pass/pallas_call | solution.py:187
  101.6 5.7 %all-to-all-start.3 = ((f32[8,8,128]{2,1,0:T(8,128)}), f32[8,8,128]{2,1,0:T(8,128)S(1)}, u32[]{:S(2)}, u32[]{:S(2)}) async-start(f32[8,8,128]{2,1,0:T(8,128)} %row_pass.3), calls=%async_computation.3 | async-start | bytes 65536 | tf_op jit(solution)/shard_map/all_to_all | solution.py:345
  107.3 0.7 bitcast_dynamic-update-slice_fusion.5
  108.0 4.0 %all-to-all-done.3.got = f32[8,8,128]{2,1,0:T(8,128)S(1)} async-done(((f32[8,8,128]{2,1,0:T(8,128)}), f32[8,8,128]{2,1,0:T(8,128)S(1)}, u32[]{:S(2)}, u32[]{:S(2)}) %all-to-all-start.3) | async-done | bytes 32800 | tf_op jit(solution)/shard_map/all_to_all | solution.py:345
  112.0 7.4 %col_pass.3 = bf16[32,8,1024]{2,1,0:T(8,128)(2,1)} custom-call(bf16[512,8192]{1,0:T(8,128)(2,1)} %get-tuple-element.13.expo, f32[8,8,128]{2,1,0:T(8,128)S(1)} %all-to-all-done.3.got), custom_call_target="tpu_custom_call" | custom-call | flops 134217728 | bytes 8388608 | tf_op jit(solution)/shard_map/col_pass/pallas_call | solution.py:217
  119.5 9.2 %all-to-all-start.4 = ((bf16[32,8,1024]{2,1,0:T(8,128)(2,1)}), bf16[32,8,1024]{2,1,0:T(8,128)(2,1)S(1)}, u32[]{:S(2)}, u32[]{:S(2)}) async-start(bf16[32,8,1024]{2,1,0:T(8,128)(2,1)} %col_pass.3), calls=%async_computation.4 | async-start | bytes 1048576 | tf_op jit(solution)/shard_map/all_to_all | solution.py:345
  128.7 0.7 bitcast_dynamic-update-slice_fusion.4
  129.4 2.4 %collective-permute-start.7 = (bf16[256,512]{1,0:T(8,128)(2,1)S(1)}, bf16[256,512]{1,0:T(8,128)(2,1)S(1)}, u32[]{:S(2)}, u32[]{:S(2)}) collective-permute-start(bf16[256,512]{1,0:T(8,128)(2,1)S(1)} %collective-permute-done.5), channel_id=1, source_target_pairs={{0,56},{8,0},{16,8},{24,16},{32,24},{40,32},{48,40},{56,48},{1,57}... | collective-permute-start | bytes 786440 | tf_op jit(solution)/shard_map/ppermute | solution.py:359
  131.9 0.7 bitcast_dynamic-update-slice_fusion.3
  132.6 0.7 bitcast_dynamic-update-slice_fusion.2
  133.3 13.8 %collective-permute-done.7 = bf16[256,512]{1,0:T(8,128)(2,1)S(1)} collective-permute-done((bf16[256,512]{1,0:T(8,128)(2,1)S(1)}, bf16[256,512]{1,0:T(8,128)(2,1)S(1)}, u32[]{:S(2)}, u32[]{:S(2)}) %collective-permute-start.7) | collective-permute-done | bytes 262176 | tf_op jit(solution)/shard_map/ppermute | solution.py:359
  147.1 0.7 bitcast_dynamic-update-slice_fusion.1
  147.8 0.4 collective-permute-done.8
  148.2 0.7 bitcast_dynamic-update-slice_fusion.mine
  148.9 1.5 collective-permute-start.9
  150.5 2.2 copy-done.1
  152.6 8.6 %last_pass.1 = (f32[64,16,128]{2,1,0:T(8,128)}, f32[512,256]{1,0:T(8,128)S(1)}, f32[8,1024]{1,0:T(8,128)S(1)}) custom-call(bf16[512,8192]{1,0:T(8,128)(2,1)} %get-tuple-element.13.expo, bf16[32,8,1024]{2,1,0:T(8,128)(2,1)S(1)} %all-to-all-done.4.got, bf16[8192,256]{1,0:T(8,128)(2,1)S(1)} %copy-done.1, bf16[512,256]{1,0:T(8,128)(2,1)S(1)} %get-tuple-element.16.unit, ...), custom_call_target="tpu_custom_call" | custom-call | flops 2147483648 | bytes 12582912 | tf_op jit(solution)/shard_map/last_pass/pallas_call | solution.py:255
  161.3 6.7 %all-to-all-start.5 = ((f32[64,16,128]{2,1,0:T(8,128)}), f32[64,16,128]{2,1,0:T(8,128)S(1)}, u32[]{:S(2)}, u32[]{:S(2)}) async-start(f32[64,16,128]{2,1,0:T(8,128)} %get-tuple-element.18), calls=%async_computation.5 | async-start | bytes 1048576 | tf_op jit(solution)/shard_map/all_to_all | solution.py:345
  168.0 17.7 %all-to-all-done.5 = f32[64,16,128]{2,1,0:T(8,128)S(1)} async-done(((f32[64,16,128]{2,1,0:T(8,128)}), f32[64,16,128]{2,1,0:T(8,128)S(1)}, u32[]{:S(2)}, u32[]{:S(2)}) %all-to-all-start.5) | async-done | bytes 524320 | tf_op jit(solution)/shard_map/all_to_all | solution.py:345
  185.7 0.2 subtract_multiply_fusion
  186.0 0.5 collective-permute-start
  186.6 0.9 collective-permute-done
  187.5 0.8 broadcast_in_dim.2
  188.3 4.0 %all-to-all-start.6 = ((bf16[4,256,256]{2,1,0:T(8,128)(2,1)}), bf16[4,256,256]{2,1,0:T(8,128)(2,1)S(1)}, u32[]{:S(2)}, u32[]{:S(2)}) async-start(bf16[4,256,256]{2,1,0:T(8,128)(2,1)} %broadcast_in_dim.2), calls=%async_computation.6 | async-start | bytes 1048576 | tf_op jit(solution)/shard_map/all_to_all | solution.py:345
  192.3 14.6 %proto_part.1 = bf16[4,256,256]{2,1,0:T(8,128)(2,1)} custom-call(s32[18]{0:T(128)S(1)} %pad_add_fusion.pos, bf16[8,256,512]{2,1,0:T(8,128)(2,1)} %bitcast_dynamic-update-slice_fusion.mine, bf16[8,256,512]{2,1,0:T(8,128)(2,1)} %collective-permute-done.9.other, f32[8,8,16,128]{3,2,1,0:T(8,128)S(1)} %bitcast.40, bf16[4,8,256,256]{3,2,1,0:T(8,128)(2,1)} %bitcast.42, ...), custom_call_target="tpu_custom_call" | custom-call | flops 6442450944 | bytes 8388608 | tf_op jit(solution)/shard_map/proto_part/pallas_call | solution.py:332
  206.9 4.0 %all-to-all-start.7 = ((bf16[4,256,256]{2,1,0:T(8,128)(2,1)}), bf16[4,256,256]{2,1,0:T(8,128)(2,1)S(1)}, u32[]{:S(2)}, u32[]{:S(2)}) async-start(bf16[4,256,256]{2,1,0:T(8,128)(2,1)} %proto_part.1), calls=%async_computation.7 | async-start | bytes 1048576 | tf_op jit(solution)/shard_map/all_to_all | solution.py:345
  210.9 1.0 collective-permute-start.1
  211.9 0.6 fusion.2
  212.5 6.6 %all-to-all-done.7 = bf16[4,256,256]{2,1,0:T(8,128)(2,1)S(1)} async-done(((bf16[4,256,256]{2,1,0:T(8,128)(2,1)}), bf16[4,256,256]{2,1,0:T(8,128)(2,1)S(1)}, u32[]{:S(2)}, u32[]{:S(2)}) %all-to-all-start.7) | async-done | bytes 524320 | tf_op jit(solution)/shard_map/all_to_all | solution.py:345
  219.2 0.7 reduce_sum.35
  219.9 0.8 maximum_select_fusion
  (31 shorter events, 0.4 us)
Async XLA Ops:
  0.6 2.2 copy-start.2
  2.8 0.9 copy-start.3
  44.8 12.7 %all-to-all-start.1 = ((f32[8,8,128]{2,1,0:T(8,128)}), f32[8,8,128]{2,1,0:T(8,128)S(1)}, u32[]{:S(2)}, u32[]{:S(2)}) async-start(f32[8,8,128]{2,1,0:T(8,128)} %row_pass.2), calls=%async_computation.1 | async-start | bytes 65536 | tf_op jit(solution)/shard_map/all_to_all | solution.py:345
  52.8 17.5 %copy-start.4 = (bf16[512,256]{1,0:T(8,128)(2,1)S(1)}, bf16[512,256]{1,0:T(8,128)(2,1)}, u32[]{:S(2)}) copy-start(bf16[512,256]{1,0:T(8,128)(2,1)} %feat.3) | copy-start | bytes 786436
  65.0 28.8 %all-to-all-start.2 = ((bf16[32,8,1024]{2,1,0:T(8,128)(2,1)}), bf16[32,8,1024]{2,1,0:T(8,128)(2,1)S(1)}, u32[]{:S(2)}, u32[]{:S(2)}) async-start(bf16[32,8,1024]{2,1,0:T(8,128)(2,1)} %col_pass.2), calls=%async_computation.2 | async-start | bytes 1048576 | tf_op jit(solution)/shard_map/all_to_all | solution.py:345
  79.6 2.0 copy-start
  82.3 8.0 %collective-permute-start.2 = (bf16[256,512]{1,0:T(8,128)(2,1)S(1)}, bf16[256,512]{1,0:T(8,128)(2,1)S(1)}, u32[]{:S(2)}, u32[]{:S(2)}) collective-permute-start(bf16[256,512]{1,0:T(8,128)(2,1)S(1)} %get-tuple-element.24), channel_id=1, source_target_pairs={{0,8},{8,16},{16,24},{24,32},{32,40},{40,48},{48,56},{56,0},{1,9},... | collective-permute-start | bytes 786440 | tf_op jit(solution)/shard_map/ppermute | solution.py:356
  83.6 7.6 %collective-permute-start.3 = (bf16[256,512]{1,0:T(8,128)(2,1)S(1)}, bf16[256,512]{1,0:T(8,128)(2,1)S(1)}, u32[]{:S(2)}, u32[]{:S(2)}) collective-permute-start(bf16[256,512]{1,0:T(8,128)(2,1)S(1)} %get-tuple-element.24), channel_id=1, source_target_pairs={{0,56},{8,0},{16,8},{24,16},{32,24},{40,32},{48,40},{56,48},{1,57}... | collective-permute-start | bytes 786440 | tf_op jit(solution)/shard_map/ppermute | solution.py:359
  90.3 17.7 %collective-permute-start.4 = (bf16[256,512]{1,0:T(8,128)(2,1)S(1)}, bf16[256,512]{1,0:T(8,128)(2,1)S(1)}, u32[]{:S(2)}, u32[]{:S(2)}) collective-permute-start(bf16[256,512]{1,0:T(8,128)(2,1)S(1)} %collective-permute-done.2), channel_id=1, source_target_pairs={{0,8},{8,16},{16,24},{24,32},{32,40},{40,48},{48,56},{56,0},{1,9},... | collective-permute-start | bytes 786440 | tf_op jit(solution)/shard_map/ppermute | solution.py:356
  91.2 38.3 %collective-permute-start.5 = (bf16[256,512]{1,0:T(8,128)(2,1)S(1)}, bf16[256,512]{1,0:T(8,128)(2,1)S(1)}, u32[]{:S(2)}, u32[]{:S(2)}) collective-permute-start(bf16[256,512]{1,0:T(8,128)(2,1)S(1)} %collective-permute-done.3), channel_id=1, source_target_pairs={{0,56},{8,0},{16,8},{24,16},{32,24},{40,32},{48,40},{56,48},{1,57}... | collective-permute-start | bytes 786440 | tf_op jit(solution)/shard_map/ppermute | solution.py:359
  101.6 10.5 %all-to-all-start.3 = ((f32[8,8,128]{2,1,0:T(8,128)}), f32[8,8,128]{2,1,0:T(8,128)S(1)}, u32[]{:S(2)}, u32[]{:S(2)}) async-start(f32[8,8,128]{2,1,0:T(8,128)} %row_pass.3), calls=%async_computation.3 | async-start | bytes 65536 | tf_op jit(solution)/shard_map/all_to_all | solution.py:345
  108.0 24.6 %collective-permute-start.6 = (bf16[256,512]{1,0:T(8,128)(2,1)S(1)}, bf16[256,512]{1,0:T(8,128)(2,1)S(1)}, u32[]{:S(2)}, u32[]{:S(2)}) collective-permute-start(bf16[256,512]{1,0:T(8,128)(2,1)S(1)} %collective-permute-done.4), channel_id=1, source_target_pairs={{0,8},{8,16},{16,24},{24,32},{32,40},{40,48},{48,56},{56,0},{1,9},... | collective-permute-start | bytes 786440 | tf_op jit(solution)/shard_map/ppermute | solution.py:356
  119.5 31.0 %all-to-all-start.4 = ((bf16[32,8,1024]{2,1,0:T(8,128)(2,1)}), bf16[32,8,1024]{2,1,0:T(8,128)(2,1)S(1)}, u32[]{:S(2)}, u32[]{:S(2)}) async-start(bf16[32,8,1024]{2,1,0:T(8,128)(2,1)} %col_pass.3), calls=%async_computation.4 | async-start | bytes 1048576 | tf_op jit(solution)/shard_map/all_to_all | solution.py:345
  129.4 17.7 %collective-permute-start.7 = (bf16[256,512]{1,0:T(8,128)(2,1)S(1)}, bf16[256,512]{1,0:T(8,128)(2,1)S(1)}, u32[]{:S(2)}, u32[]{:S(2)}) collective-permute-start(bf16[256,512]{1,0:T(8,128)(2,1)S(1)} %collective-permute-done.5), channel_id=1, source_target_pairs={{0,56},{8,0},{16,8},{24,16},{32,24},{40,32},{48,40},{56,48},{1,57}... | collective-permute-start | bytes 786440 | tf_op jit(solution)/shard_map/ppermute | solution.py:359
  132.6 15.6 %collective-permute-start.8 = (bf16[256,512]{1,0:T(8,128)(2,1)S(1)}, bf16[256,512]{1,0:T(8,128)(2,1)S(1)}, u32[]{:S(2)}, u32[]{:S(2)}) collective-permute-start(bf16[256,512]{1,0:T(8,128)(2,1)S(1)} %collective-permute-done.6), channel_id=1, source_target_pairs={{0,8},{8,16},{16,24},{24,32},{32,40},{40,48},{48,56},{56,0},{1,9},... | collective-permute-start | bytes 786440 | tf_op jit(solution)/shard_map/ppermute | solution.py:356
  148.9 43.4 %collective-permute-start.9 = (bf16[8,256,512]{2,1,0:T(8,128)(2,1)}, bf16[8,256,512]{2,1,0:T(8,128)(2,1)}, u32[]{:S(2)}, u32[]{:S(2)}) collective-permute-start(bf16[8,256,512]{2,1,0:T(8,128)(2,1)} %bitcast_dynamic-update-slice_fusion.mine), channel_id=1, source_target_pairs={{0,1},{1,0},{2,3},{3,2},{4,5},{5,4},{6,7},{7,6},{8,9},{9,8},{10,11... | collective-permute-start | bytes 6291464 | tf_op jit(solution)/shard_map/ppermute | solution.py:349
  150.5 2.2 copy-start.1
  152.6 15.4 %copy-start.5 = (s32[8]{0:T(128)S(1)}, s32[8]{0:T(128)}, u32[]{:S(2)}) copy-start(s32[8]{0:T(128)} %constant.48.clone) | copy-start | bytes 100
  161.3 24.4 %all-to-all-start.5 = ((f32[64,16,128]{2,1,0:T(8,128)}), f32[64,16,128]{2,1,0:T(8,128)S(1)}, u32[]{:S(2)}, u32[]{:S(2)}) async-start(f32[64,16,128]{2,1,0:T(8,128)} %get-tuple-element.18), calls=%async_computation.5 | async-start | bytes 1048576 | tf_op jit(solution)/shard_map/all_to_all | solution.py:345
  186.0 1.5 collective-permute-start
  188.3 18.6 %all-to-all-start.6 = ((bf16[4,256,256]{2,1,0:T(8,128)(2,1)}), bf16[4,256,256]{2,1,0:T(8,128)(2,1)S(1)}, u32[]{:S(2)}, u32[]{:S(2)}) async-start(bf16[4,256,256]{2,1,0:T(8,128)(2,1)} %broadcast_in_dim.2), calls=%async_computation.6 | async-start | bytes 1048576 | tf_op jit(solution)/shard_map/all_to_all | solution.py:345
  206.9 12.3 %all-to-all-start.7 = ((bf16[4,256,256]{2,1,0:T(8,128)(2,1)}), bf16[4,256,256]{2,1,0:T(8,128)(2,1)S(1)}, u32[]{:S(2)}, u32[]{:S(2)}) async-start(bf16[4,256,256]{2,1,0:T(8,128)(2,1)} %proto_part.1), calls=%async_computation.7 | async-start | bytes 1048576 | tf_op jit(solution)/shard_map/all_to_all | solution.py:345
  210.9 9.0 %collective-permute-start.1 = (bf16[256,256]{1,0:T(8,128)(2,1)S(1)}, bf16[256,256]{1,0:T(8,128)(2,1)S(1)}, u32[]{:S(2)}, u32[]{:S(2)}) collective-permute-start(bf16[256,256]{1,0:T(8,128)(2,1)S(1)} %reduce_sum.34), channel_id=1, source_target_pairs={{0,1},{1,0},{2,3},{3,2},{4,5},{5,4},{6,7},{7,6},{8,9},{9,8},{10,11... | collective-permute-start | bytes 393224 | tf_op jit(solution)/shard_map/ppermute | solution.py:349

commit v2 on v0

v2 whole, which is shorter than its diff:
```python
import math

import jax
import jax.numpy as jnp
from jax import lax
from jax.experimental import pallas as pl
from jax.experimental.pallas import tpu as pltpu
from jax.sharding import Mesh, PartitionSpec as P

f32 = jnp.float32
bf16 = jnp.bfloat16

NX, NZ, NY, NC = 4, 8, 4, 2
DIM = 256
PROTOS = 65536
BATCH = 16384
ROWS = BATCH // (NX * NZ)
COLS = PROTOS // (NY * NC)
BK = 1024
NB = COLS // BK
T_EXP2 = math.log2(math.e) / 0.07
S_EXP2 = math.log2(math.e) / 0.1
FACTOR = PROTOS / (BATCH * 0.1)
VMEM = 60 * 1024 * 1024
SMALL = 24 * 1024 * 1024

NT = (((1,), (1,)), ((), ()))
NN = (((1,), (0,)), ((), ()))


def dot(a, b, dims):
    return lax.dot_general(a, b, dims, preferred_element_type=f32)


def unit_rows(x):
    xf = x.astype(f32)
    return (xf * lax.rsqrt(jnp.sum(xf * xf, axis=1, keepdims=True) + 1e-06)).astype(bf16)


def lane_fold(m):
    acc = m[:, :128]
    for i in range(1, m.shape[1] // 128):
        acc = acc + m[:, i * 128 : (i + 1) * 128]
    return acc


def to_lanes(acc):
    return jnp.sum(acc.T, axis=0, keepdims=True)


def rows4(v):
    return jnp.concatenate([v[:, i * 128 : (i + 1) * 128] for i in range(4)], axis=0)


def lanes512(m):
    return jnp.concatenate([m[i : i + 1] for i in range(4)], axis=1)


def call(kernel, ins, outs, out_shape, scratch, flops, nbytes, name, limit=VMEM):
    return pl.pallas_call(
        kernel,
        in_specs=ins,
        out_specs=outs,
        out_shape=out_shape,
        scratch_shapes=scratch,
        compiler_params=pltpu.CompilerParams(vmem_limit_bytes=limit),
        cost_estimate=pl.CostEstimate(flops=flops, bytes_accessed=nbytes, transcendentals=0),
        name=name,
    )


ANY = pl.BlockSpec(memory_space=pl.ANY)
INSIDE = pl.BlockSpec(memory_space=pltpu.VMEM)
SCALARS = pl.BlockSpec(memory_space=pltpu.SMEM)
DMA = pltpu.SemaphoreType.DMA


def begin(src, dst, sem):
    copy = pltpu.make_async_copy(src, dst, sem)
    copy.start()
    return copy


def begin_blocks(src, dst, sems):
    for j in range(NB):
        begin(src.at[j], dst.at[j], sems.at[j])


def shape(s, t):
    return jax.ShapeDtypeStruct(s, t)


def teacher_kernel(feat, protos, expo_o, cols_o, feat_s, protos_s, expo_s, logit_s, cols_s, sem, in_sems, out_sems):
    first = begin(feat, feat_s, sem)
    begin_blocks(protos, protos_s, in_sems)
    first.wait()
    feat_s[...] = unit_rows(feat_s[...])

    @pl.loop(0, NB)
    def _(j):
        pltpu.make_async_copy(protos.at[j], protos_s.at[j], in_sems.at[j]).wait()
        sums = []
        for n in range(BK // DIM):
            logit_s[n] = dot(feat_s[...], unit_rows(protos_s[j, n * DIM : (n + 1) * DIM, :]), NT)
            acc = jnp.zeros((8, DIM), f32)
            for r in range(0, ROWS, 64):
                e = jnp.exp2(logit_s[n, r : r + 64, :] * T_EXP2)
                expo_s[j, r : r + 64, n * DIM : (n + 1) * DIM] = e.astype(bf16)
                for q in range(0, 64, 8):
                    acc = acc + e[q : q + 8]
            sums.append(jnp.sum(acc, axis=0, keepdims=True))
        cols_s[pl.ds(j, 1), :] = jnp.concatenate(sums, axis=1)
        pltpu.make_async_copy(expo_s.at[j], expo_o.at[j], out_sems.at[j]).start()

    cols_o[...] = jnp.broadcast_to(cols_s[...].astype(bf16)[None], cols_o.shape)
    for j in range(NB):
        pltpu.make_async_copy(expo_s.at[j], expo_o.at[j], out_sems.at[j]).wait()


def teacher(feat, protos):
    return call(
        teacher_kernel,
        [ANY, ANY],
        [ANY, INSIDE],
        [shape((NB, ROWS, BK), bf16), shape((NX * NZ, NB, BK), bf16)],
        [
            pltpu.VMEM((ROWS, DIM), bf16),
            pltpu.VMEM((NB, BK, DIM), bf16),
            pltpu.VMEM((NB, ROWS, BK), bf16),
            pltpu.VMEM((BK // DIM, ROWS, DIM), f32),
            pltpu.VMEM((NB, BK), f32),
            DMA,
            DMA((NB,)),
            DMA((NB,)),
        ],
        2 * ROWS * COLS * DIM,
        ROWS * COLS * 2 + COLS * DIM * 2,
        "teacher",
    )(feat, protos.reshape(NB, BK, DIM))


def student_kernel(
    feat, protos, dirs_o, tot_o, mix_o, feat_s, protos_s, dirs_s, logit_s, exp_s, tot_s, sem, in_sems, out_sems
):
    first = begin(feat, feat_s, sem)
    begin_blocks(protos, protos_s, in_sems)
    first.wait()
    feat_s[...] = unit_rows(feat_s[...])
    tot_s[...] = jnp.zeros_like(tot_s)
    mix_o[...] = jnp.zeros_like(mix_o)

    @pl.loop(0, NB)
    def _(j):
        pltpu.make_async_copy(protos.at[j], protos_s.at[j], in_sems.at[j]).wait()
        for n in range(BK // DIM):
            part = slice(n * DIM, (n + 1) * DIM)
            dirs = unit_rows(protos_s[j, part, :])
            dirs_s[j, part, :] = dirs
            logit_s[n] = dot(feat_s[...], dirs, NT)
            for r in range(0, ROWS, 64):
                e = jnp.exp2(logit_s[n, r : r + 64, :] * S_EXP2)
                exp_s[r : r + 64, part] = e.astype(bf16)
                tot_s[r : r + 64, :] += lane_fold(e)
        mix_o[...] += dot(exp_s[...], dirs_s[j], NN)
        pltpu.make_async_copy(dirs_s.at[j], dirs_o.at[j], out_sems.at[j]).start()

    tot_o[...] = rows4(to_lanes(tot_s[...]))
    for j in range(NB):
        pltpu.make_async_copy(dirs_s.at[j], dirs_o.at[j], out_sems.at[j]).wait()


def student(feat, protos):
    return call(
        student_kernel,
        [ANY, ANY],
        [ANY, INSIDE, INSIDE],
        [shape((NB, BK, DIM), bf16), shape((4, 128), f32), shape((ROWS, DIM), f32)],
        [
            pltpu.VMEM((ROWS, DIM), bf16),
            pltpu.VMEM((NB, BK, DIM), bf16),
            pltpu.VMEM((NB, BK, DIM), bf16),
            pltpu.VMEM((BK // DIM, ROWS, DIM), f32),
            pltpu.VMEM((ROWS, BK), bf16),
            pltpu.VMEM((ROWS, 128), f32),
            DMA,
            DMA((NB,)),
            DMA((NB,)),
        ],
        4 * ROWS * COLS * DIM,
        COLS * DIM * 4,
        "student",
    )(feat, protos.reshape(NB, BK, DIM))


def col_scale(got):
    return 1.0 / (PROTOS * jnp.sum(got[...].astype(f32), axis=0))


def scaled_rows(expo, col, acc_s, j):
    c = col[pl.ds(j, 1), :]
    cs = [c[:, g * 128 : (g + 1) * 128] for g in range(BK // 128)]
    for r in range(0, ROWS, 32):
        acc = acc_s[r : r + 32, :]
        for g in range(BK // 128):
            acc = acc + expo[j, r : r + 32, g * 128 : (g + 1) * 128].astype(f32) * cs[g]
        acc_s[r : r + 32, :] = acc


def row_last_kernel(expo, got, rows_o, col_o, expo_s, got_s, acc_s, sem, sems):
    first = begin(got, got_s, sem)
    begin_blocks(expo, expo_s, sems)
    acc_s[...] = jnp.zeros_like(acc_s)
    first.wait()
    col_o[...] = col_scale(got_s)

    @pl.loop(0, NB)
    def _(j):
        pltpu.make_async_copy(expo.at[j], expo_s.at[j], sems.at[j]).wait()
        scaled_rows(expo_s, col_o, acc_s, j)

    rows_o[...] = jnp.broadcast_to(rows4(to_lanes(acc_s[...]))[None], rows_o.shape)


def row_last(expo, got):
    return call(
        row_last_kernel,
        [ANY, ANY],
        [INSIDE, INSIDE],
        [shape((NZ * NY * NC, 4, 128), f32), shape((NB, BK), f32)],
        [
            pltpu.VMEM((NB, ROWS, BK), bf16),
            pltpu.VMEM(got.shape, bf16),
            pltpu.VMEM((ROWS, 128), f32),
            DMA,
            DMA((NB,)),
        ],
        2 * ROWS * COLS,
        ROWS * COLS * 2,
        "row_last",
    )(expo, got)


def row_kernel(expo, got, tot, rows_o, got_s, col_s, acc_s, sem):
    first = begin(got, got_s, sem)
    acc_s[...] = jnp.zeros_like(acc_s)
    first.wait()
    col_s[...] = col_scale(got_s[:, :, :BK])

    @pl.loop(0, NB)
    def _(j):
        scaled_rows(expo, col_s, acc_s, j)

    part = jnp.concatenate([rows4(to_lanes(acc_s[...])), tot[...]], axis=0)
    rows_o[...] = jnp.broadcast_to(part[None], rows_o.shape)


def row_pass(held, got, tot):
    return call(
        row_kernel,
        [INSIDE, ANY, INSIDE],
        INSIDE,
        shape((NY * NC, 8, 128), f32),
        [pltpu.VMEM(got.shape, bf16), pltpu.VMEM((NB, BK), f32), pltpu.VMEM((ROWS, 128), f32), DMA],
        2 * ROWS * COLS,
        1 << 16,
        "row_pass",
        SMALL,
    )(pltpu.with_memory_space_constraint(held, pltpu.VMEM), got, tot)


def col_kernel(expo, got, cols_o, tot_o, scale_s, cols_s):
    total = jnp.sum(got[...], axis=0)
    scale_s[...] = jnp.broadcast_to(1.0 / (BATCH * lanes512(total[:4])), (128, ROWS)).T

    @pl.loop(0, NB)
    def _(j):
        accs = [jnp.zeros((8, 128), f32)] * (BK // 128)
        for r in range(0, ROWS, 32):
            scale = scale_s[r : r + 32, :]
            for g in range(BK // 128):
                t = expo[j, r : r + 32, g * 128 : (g + 1) * 128].astype(f32) * scale
                accs[g] = accs[g] + ((t[0:8] + t[8:16]) + (t[16:24] + t[24:32]))
        cols_s[pl.ds(j, 1), :] = jnp.concatenate(
            [jnp.sum(a, axis=0, keepdims=True) for a in accs], axis=1
        )

    cols_o[...] = jnp.broadcast_to(cols_s[...].astype(bf16)[None], cols_o.shape)
    hi = total[4:].astype(bf16).astype(f32)
    tot_o[...] = jnp.concatenate([hi, total[4:] - hi], axis=0).astype(bf16)


def col_pass(held, got, copies):
    return call(
        col_kernel,
        [INSIDE, INSIDE],
        [INSIDE, INSIDE],
        [shape((copies, NB, BK), bf16), shape((8, 128), bf16)],
        [pltpu.VMEM((ROWS, 128), f32), pltpu.VMEM((NB, BK), f32)],
        2 * ROWS * COLS,
        1 << 20,
        "col_pass",
        SMALL,
    )(pltpu.with_memory_space_constraint(held, pltpu.VMEM), got)


def mix_kernel(expo, col, dirs, feat, mix_o, cross_o, expo_s, dirs_s, feat_s, w_s, sem, sems):
    for j in range(NB):
        begin(expo.at[j], expo_s.at[j], sems.at[0, j])
        begin(dirs.at[j], dirs_s.at[j], sems.at[1, j])
    first = begin(feat, feat_s, sem)
    mix_o[...] = jnp.zeros_like(mix_o)

    @pl.loop(0, NB)
    def _(j):
        pltpu.make_async_copy(expo.at[j], expo_s.at[j], sems.at[0, j]).wait()
        c = col[pl.ds(j, 1), :]
        cs = [c[:, g * 128 : (g + 1) * 128] for g in range(BK // 128)]
        for r in range(0, ROWS, 32):
            for g in range(BK // 128):
                part = slice(g * 128, (g + 1) * 128)
                w_s[r : r + 32, part] = (expo_s[j, r : r + 32, part].astype(f32) * cs[g]).astype(bf16)
        pltpu.make_async_copy(dirs.at[j], dirs_s.at[j], sems.at[1, j]).wait()
        mix_o[...] += dot(w_s[...], dirs_s[j], NN)

    first.wait()
    unit = unit_rows(feat_s[...]).astype(f32)
    cross_o[...] = to_lanes(lane_fold(mix_o[...] * unit)) / 0.1


def mix_pass(expo, col, dirs, feat):
    return call(
        mix_kernel,
        [ANY, INSIDE, ANY, ANY],
        [INSIDE, INSIDE],
        [shape((ROWS, DIM), f32), shape((1, ROWS), f32)],
        [
            pltpu.VMEM((NB, ROWS, BK), bf16),
            pltpu.VMEM((NB, BK, DIM), bf16),
            pltpu.VMEM((ROWS, DIM), bf16),
            pltpu.VMEM((ROWS, BK), bf16),
            DMA,
            DMA((2, NB)),
        ],
        2 * ROWS * COLS * DIM,
        ROWS * COLS * 2 + COLS * DIM * 2,
        "mix_pass",
    )(expo, col, dirs, feat)


def early_kernel(*refs):
    pos, mine, other = refs[0], refs[1 : 1 + NZ], refs[1 + NZ : 1 + 2 * NZ]
    (t_protos, s_dirs, got, rows_o, dirs_o, grad_o,
     raw_s, rows_s, t_s, s_s, got_s, d_s, small, sems, outs) = refs[1 + 2 * NZ :]
    z, core = pos[0], pos[1]
    for k in range(NZ):
        begin(mine[k], raw_s.at[k, core], sems.at[0, k])
        begin(other[k], raw_s.at[k, 1 - core], sems.at[1, k])
        if k == 0:
            first = [begin(t_protos.at[i, z], t_s.at[pl.ds(i * DIM, DIM)], small.at[i]) for i in range(NX)]
            first += [begin(s_dirs.at[i, z], s_s.at[pl.ds(i * DIM, DIM)], small.at[NX + i]) for i in range(NX)]
            first.append(begin(got, got_s, small.at[2 * NX]))
    grad_o[...] = jnp.zeros_like(grad_o)
    for copy in first:
        copy.wait()
    dirs_o[...] = unit_rows(t_s[...])

    @pl.loop(0, NZ)
    def _(k):
        pltpu.make_async_copy(mine[0], raw_s.at[k, core], sems.at[0, k]).wait()
        pltpu.make_async_copy(other[0], raw_s.at[k, 1 - core], sems.at[1, k]).wait()
        total = got_s[pos[3 + k]].astype(f32)[:, BK:]
        scale = FACTOR / lanes512(total[:4] + total[4:])
        half = ROWS // NC
        for h in range(NC):
            part = slice(h * half, (h + 1) * half)
            rows_s[k, part, :DIM] = unit_rows(raw_s[k, h, :, :DIM])
            rows_s[k, part, DIM:] = unit_rows(raw_s[k, h, :, DIM:])
        pltpu.make_async_copy(rows_s.at[k], rows_o.at[k], outs.at[k]).start()
        s_rows = rows_s[k, :, DIM:]
        d_s[...] = (jnp.exp2(dot(s_s[...], s_rows, NT) * S_EXP2) * scale).astype(bf16)
        grad_o[...] += dot(d_s[...], s_rows, NN)

    for k in range(NZ):
        pltpu.make_async_copy(rows_s.at[k], rows_o.at[k], outs.at[k]).wait()


def early(pos, mine, other, t_protos, s_dirs, got):
    n, half = NX * DIM, ROWS // NC
    return call(
        early_kernel,
        [SCALARS] + [ANY] * (2 * NZ + 3),
        [ANY, INSIDE, INSIDE],
        [shape((NZ, ROWS, 2 * DIM), bf16), shape((n, DIM), bf16), shape((n, DIM), f32)],
        [
            pltpu.VMEM((NZ, NC, half, 2 * DIM), bf16),
            pltpu.VMEM((NZ, ROWS, 2 * DIM), bf16),
            pltpu.VMEM((n, DIM), bf16),
            pltpu.VMEM((n, DIM), bf16),
            pltpu.VMEM(got.shape, bf16),
            pltpu.VMEM((n, ROWS), bf16),
            DMA((2 * NX + 1,)),
            DMA((2, NZ)),
            DMA((NZ,)),
        ],
        4 * ROWS * COLS * DIM,
        ROWS * COLS,
        "early",
    )(pos, *mine, *other, t_protos, s_dirs, got)


def down_rows(v):
    return jnp.broadcast_to(v, (128, v.shape[1])).T


def scale_rows(m, scale):
    return jnp.concatenate([m[:, g : g + 128] * scale for g in range(0, m.shape[1], 128)], axis=1)


def grad_kernel(
    pos, dirs, rows, stat, got, student_part, col, s_mix, t_mix, cross,
    own_o, next_o, keep_o, give_o, line_o,
    rows_s, stat_s, got_s, dirs_s, part_s, acc_s, s_mix_s, t_mix_s, small, sems,
):
    z, core, x = pos[0], pos[1], pos[2]
    first = [begin(stat, stat_s, small.at[0]), begin(dirs, dirs_s, small.at[1])]
    for k in range(NZ):
        begin(rows.at[k], rows_s.at[k], sems.at[k])
    second = [
        begin(got.at[pl.ds(z, 1)], got_s, small.at[2]),
        begin(s_mix, s_mix_s, small.at[3]),
        begin(t_mix, t_mix_s, small.at[4]),
        begin(student_part, part_s, small.at[5]),
    ]
    acc_s[...] = jnp.zeros_like(acc_s)
    for copy in first:
        copy.wait()

    @pl.loop(0, NZ)
    def _(k):
        total = jnp.sum(stat_s[pos[3 + k]], axis=0)
        scale = down_rows(FACTOR / lanes512(total))
        pltpu.make_async_copy(rows.at[k], rows_s.at[k], sems.at[k]).wait()
        expo = jnp.exp2(dot(dirs_s[...], rows_s[k, :, :DIM], NT) * T_EXP2).astype(bf16)
        r = scale_rows(rows_s[k, :, DIM:].astype(f32), scale).astype(bf16)
        acc_s[...] += dot(expo, r, NN)

    for copy in second:
        copy.wait()
    for d in range(NX):
        i = lax.rem(x + d, NX)
        c = col[pl.ds(2 * i + z // 4, 1), :]
        c = sum(jnp.where(lax.rem(z, 4) == q, c[:, q * DIM : (q + 1) * DIM], 0.0) for q in range(4))
        part = pl.ds(pl.multiple_of(i * DIM, DIM), DIM)
        block = part_s[part, :] - scale_rows(acc_s[part, :], down_rows(c))
        if d == 0:
            own_o[...] = block
        else:
            next_o[d - 1] = block.astype(bf16)

    row_total = lanes512(jnp.sum(stat_s[z], axis=0))
    total = got_s[0].astype(f32)[:, BK:]
    total = lanes512(total[:4] + total[4:])
    s_mix_s[...] = scale_rows(s_mix_s[...], down_rows(FACTOR / total)) - scale_rows(
        t_mix_s[...], down_rows(FACTOR / row_total)
    )
    half = ROWS // NC
    keep_o[:half, :] = s_mix_s[pl.ds(pl.multiple_of(core * half, half), half), :]
    give_o[:half, :] = s_mix_s[pl.ds(pl.multiple_of((1 - core) * half, half), half), :].astype(bf16)
    loss = cross[...] / row_total
    low, high = loss[:, :half], loss[:, half:]
    away = jnp.where(core == 0, high, low)
    hi = away.astype(bf16).astype(f32)
    zeros = jnp.zeros((14, DIM), f32)
    give_o[half:, :] = jnp.concatenate([hi, away - hi, zeros], axis=0).astype(bf16)
    keep_o[half:, :] = jnp.concatenate([jnp.where(core == 0, low, high), zeros[:7]], axis=0)
    line_o[...] = jnp.log(total)


def proto_part(pos, dirs, rows, stat, got, student_part, col, s_mix, t_mix, cross):
    n, half = NX * DIM, ROWS // NC
    return call(
        grad_kernel,
        [SCALARS, ANY, ANY, ANY, ANY, ANY, INSIDE, ANY, ANY, INSIDE],
        [INSIDE] * 5,
        [
            shape((DIM, DIM), f32),
            shape((NX - 1, DIM, DIM), bf16),
            shape((half + 8, DIM), f32),
            shape((half + 16, DIM), bf16),
            shape((1, ROWS), f32),
        ],
        [
            pltpu.VMEM((NZ, ROWS, 2 * DIM), bf16),
            pltpu.VMEM((NZ, NY * NC, 4, 128), f32),
            pltpu.VMEM((1,) + got.shape[1:], bf16),
            pltpu.VMEM((n, DIM), bf16),
            pltpu.VMEM((n, DIM), f32),
            pltpu.VMEM((n, DIM), f32),
            pltpu.VMEM((ROWS, DIM), f32),
            pltpu.VMEM((ROWS, DIM), f32),
            DMA((6,)),
            DMA((NZ,)),
        ],
        4 * ROWS * COLS * DIM,
        ROWS * COLS,
        "proto_part",
    )(pos, dirs, rows, stat, got, student_part, col, s_mix, t_mix, cross)


def gather(a, axes):
    return lax.all_to_all(a, axes, 0, 0)


def swap_core(a):
    return lax.ppermute(a, "c", [(0, 1), (1, 0)])


def shift(a, axis, by):
    n = lax.axis_size(axis)
    return lax.ppermute(a, axis, [(i, (i + by) % n) for i in range(n)])


OFFSETS = (0, -1, 1, -2, 2, -3, 3, -4)


def packed(terms, loss):
    hi = lax.reduce_precision(loss, 8, 7)
    tail = jnp.concatenate([hi, loss - hi, jnp.zeros((14, DIM), f32)], axis=0)
    return jnp.concatenate([terms, tail], axis=0).astype(bf16)


def unpacked(a):
    a = a.astype(f32)
    n = a.shape[0] - 16
    return a[:n], a[n : n + 1] + a[n + 1 : n + 2]


def around(a, axis):
    one, two, three = [shift(a, axis, d).astype(f32) for d in (1, 2, 3)]
    return (a.astype(f32) + two) + (one + three)


def local(teacher_feat, student_feat, teacher_protos, student_protos):
    z = lax.axis_index("z")
    core = lax.axis_index("c")
    half = ROWS // NC
    together = lax.optimization_barrier

    def my_half(a):
        return lax.dynamic_slice_in_dim(a, core * half, half, 0)

    order = (z + jnp.array(OFFSETS, jnp.int32)) % NZ
    pos = jnp.concatenate([jnp.stack([z, core, lax.axis_index("x")]), order]).astype(jnp.int32)

    b0 = jnp.concatenate([my_half(teacher_feat), my_half(student_feat)], axis=1)
    u1, d1 = shift(b0, "z", 1), shift(b0, "z", -1)
    expo, cols = teacher(teacher_feat, teacher_protos)
    cols, u1, d1 = together((cols, u1, d1))

    u2, d2 = shift(u1, "z", 1), shift(d1, "z", -1)
    o0 = swap_core(b0)
    got = gather(cols, ("x", "z"))
    s_dirs, tot, s_mix = student(student_feat, student_protos)
    got, u2, d2, o0, tot = together((got, u2, d2, o0, tot))

    u3, d3 = shift(u2, "z", 1), shift(d2, "z", -1)
    ou1, od1, ou2, od2 = [swap_core(a) for a in (u1, d1, u2, d2)]
    rows = row_pass(expo, got, tot)
    got = gather(rows, ("y", "c"))
    got, u3, d3, ou1, od1, ou2, od2 = together((got, u3, d3, ou1, od1, ou2, od2))

    cols, tots = col_pass(expo, got, 1)
    cols = around(cols[0], "x").astype(bf16)
    cols = jnp.concatenate([cols, tots], axis=1)
    got2 = gather(jnp.broadcast_to(cols[None], (NZ,) + cols.shape), "z")

    u4 = shift(u3, "z", 1)
    ou3, od3 = swap_core(u3), swap_core(d3)
    rows = row_pass(expo, got2, tot)
    got = gather(rows, ("y", "c"))
    got, u4, ou3, od3 = together((got, u4, ou3, od3))

    ou4 = swap_core(u4)
    cols, _ = col_pass(expo, got, NX * NZ)
    cols, ou4 = together((cols, ou4))
    got = gather(cols, ("x", "z"))
    rows_c, dirs_c, student_part = early(
        pos,
        [b0, u1, d1, u2, d2, u3, d3, u4],
        [o0, ou1, od1, ou2, od2, ou3, od3, ou4],
        teacher_protos.reshape(NX, NZ, DIM, DIM),
        s_dirs.reshape(NX, NZ, DIM, DIM),
        got2,
    )
    got, student_part = together((got, student_part))

    rows, col = row_last(expo, got)
    rows, col = together((rows, col))
    stat = gather(rows, ("z", "y", "c")).reshape(NZ, NY * NC, 4, 128)
    t_mix, cross = mix_pass(expo, col, s_dirs, student_feat)
    stat, t_mix, cross = together((stat, t_mix, cross))
    own, following, keep, give, log_total = proto_part(
        pos, dirs_c, rows_c, stat, got2, student_part, col, s_mix, t_mix, cross
    )
    arrived = [shift(following[d], "x", d + 1).astype(f32) for d in range(NX - 1)]
    proto_grad = ((own + arrived[0]) + (arrived[1] + arrived[2])).astype(bf16)

    terms, loss = unpacked(swap_core(give))
    mine = packed(keep[:half] + terms, keep[half : half + 1] + loss)
    terms, loss = unpacked(mine)
    away = [unpacked(shift(mine, "y", d)) for d in (1, 2, 3)]
    terms = (terms + away[1][0]) + (away[0][0] + away[2][0])
    loss = (loss + away[1][1]) + (away[0][1] + away[2][1])
    done = packed(terms, loss)
    there = swap_core(done)
    low, low_loss = unpacked(jnp.where(core == 0, done, there))
    high, high_loss = unpacked(jnp.where(core == 0, there, done))
    feature_grad = jnp.concatenate([low, high], axis=0).astype(bf16)
    row_loss = (log_total - jnp.concatenate([low_loss, high_loss], axis=1)).reshape(ROWS)
    return row_loss, feature_grad, proto_grad


def solution(mesh):
    fine = Mesh(mesh.devices.reshape(NX, NZ, NY, NC), ("x", "z", "y", "c"))
    rows, protos = P(("x", "z"), None), P(("y", "c"), None)
    return jax.shard_map(
        local,
        mesh=fine,
        in_specs=(rows, rows, protos, protos),
        out_specs=(P(("x", "z")), rows, P(("y", "c", "x", "z"), None)),
        check_vma=False,
    )
```

time: 849 us -> 196 us (0.23)
  blocking collectives: 501 us -> 0 us
  waiting for transfers between devices: 180 us -> 25.7 us
  matrix products: 115 us -> 0 us
  starting transfers between devices: 0.04 us -> 74.1 us
  Pallas kernels: 0 us -> 68.9 us
  other arithmetic: 23.3 us -> 4.96 us
  between operations: 14.4 us -> 1.18 us
  local copies, waits for them, and re-layouts: 8.92 us -> 18.8 us
    psum x8 -> x0, blocking collectives: 501 us -> none  [the longest x3 340 us: local(): col_whole = lax.psum(local_col, 'dp')]
    reduce_scatter x1 -> x0, waiting for transfers between devices: 180 us -> none  [local(): lax.psum_scatter(by_cols(dlog, s_unit), 'dp', scatter_dimension=0, tiled=...]
    dot_general x10 -> x0, matrix products: 115 us -> none  [the longest x3 52.9 us: local(): jnp.dot(expo, col_scale, precision=lax.Precision.HIGHEST, preferred_eleme...]
    pallas_call x0 -> x10, Pallas kernels: none -> 68.9 us  [the longest x1 13.1 us: early(): call(early_kernel, [SCALARS] + [ANY] * (2 * NZ + 3), [ANY, INSIDE, INSIDE...]
    all_to_all x0 -> x6, starting transfers between devices: none -> 38.7 us  [gather(): return lax.all_to_all(a, axes, 0, 0)]
    ppermute x0 -> x26, starting transfers between devices: none -> 35.4 us  [the longest x16 25.4 us: shift(): return lax.ppermute(a, axis, [(i, (i + by) % n) for i in range(n)])]
    all_to_all x0 -> x6, waiting for transfers between devices: none -> 17.1 us  [gather(): return lax.all_to_all(a, axes, 0, 0)]
    convert_element_type x2 -> x8, other arithmetic: 13.7 us -> 1.06 us  [the longest x1 0.72 us: local(): proto_grad = (own + arrived[0] + (arrived[1] + arrived[2])).astype(bf16)]
  transfers between devices with their start and end apart: 1 -> 32, of which waited for: 1 -> 11; matrix products, arithmetic and copies ran while one was open for 1% -> 1% of each run, Pallas kernels for 0% -> 25%
where the time goes in v2:
time: 196 us; the launch traced here: 194 us
  starting transfers between devices  74.1 us (38%)
  Pallas kernels  68.9 us (35%)
  waiting for transfers between devices  25.7 us (13%)
  local copies, waits for them, and re-layouts  18.8 us (10%)
  other arithmetic  4.96 us (3%)
    all_to_all x6, starting transfers between devices, gather(): return lax.all_to_all(a, axes, 0, 0)  38.7 us
    ppermute x16, starting transfers between devices, shift(): return lax.ppermute(a, axis, [(i, (i + by) % n) for i in range(n)])  25.4 us
    all_to_all x6, waiting for transfers between devices, gather(): return lax.all_to_all(a, axes, 0, 0)  17.1 us
    unnamed x56, local copies, waits for them, and re-layouts  16 us
    pallas_call x1, Pallas kernels, early(): call(early_kernel, [SCALARS] + [ANY] * (2 * NZ + 3), [ANY, INSIDE, INSIDE...  13.1 us
    pallas_call x1, Pallas kernels, proto_part(): call(grad_kernel, [SCALARS, ANY, ANY, ANY, ANY, ANY, INSIDE, ANY, ANY, IN...  11.7 us
    pallas_call x1, Pallas kernels, student(): call(student_kernel, [ANY, ANY], [ANY, INSIDE, INSIDE], [shape((NB, BK, D...  11.1 us
    ppermute x10, starting transfers between devices, swap_core(): return lax.ppermute(a, 'c', [(0, 1), (1, 0)])  10 us
  transfers between devices with their start and end apart: 32, of which 11 were waited for; matrix products, arithmetic and copies ran while one was open for 1% of the time, Pallas kernels for 25%

profile of v2, /device:TPU:1, one launch (start us, length us, event | category | flops | bytes accessed | tf_op | source)
XLA Modules:
  0.0 193.7 jit_solution(14319051046061117705)
XLA Ops:
  0.6 1.0 constant_dynamic-slice_fusion
  1.7 2.5 %collective-permute-start = (bf16[256,512]{1,0:T(8,128)(2,1)S(1)}, bf16[256,512]{1,0:T(8,128)(2,1)S(1)}, u32[]{:S(2)}, u32[]{:S(2)}) collective-permute-start(bf16[256,512]{1,0:T(8,128)(2,1)S(1)} %pad_maximum_fusion.refs_1_), channel_id=1, source_target_pairs={{0,8},{8,16},{16,24},{24,32},{32,40},{40,48},{48,56},{56,0},{1,9},... | collective-permute-start | bytes 786440 | tf_op jit(solution)/shard_map/ppermute | solution.py:520
  4.2 4.0 %collective-permute-start.1 = (bf16[256,512]{1,0:T(8,128)(2,1)S(1)}, bf16[256,512]{1,0:T(8,128)(2,1)S(1)}, u32[]{:S(2)}, u32[]{:S(2)}) collective-permute-start(bf16[256,512]{1,0:T(8,128)(2,1)S(1)} %pad_maximum_fusion.refs_1_), channel_id=1, source_target_pairs={{0,56},{8,0},{16,8},{24,16},{32,24},{40,32},{48,40},{56,48},{1,57}... | collective-permute-start | bytes 786440 | tf_op jit(solution)/shard_map/ppermute | solution.py:520
  8.2 9.0 %teacher.1 = (bf16[8,512,1024]{2,1,0:T(8,128)(2,1)}, bf16[32,8,1024]{2,1,0:T(8,128)(2,1)}) custom-call(bf16[512,256]{1,0:T(8,128)(2,1)} %feat.3, bf16[8,1024,256]{2,1,0:T(8,128)(2,1)} %bitcast.24), custom_call_target="tpu_custom_call" | custom-call | flops 2147483648 | bytes 12582912 | tf_op jit(solution)/shard_map/teacher/pallas_call | solution.py:121
  17.3 8.1 %all-to-all-start = ((bf16[32,8,1024]{2,1,0:T(8,128)(2,1)}), bf16[32,8,1024]{2,1,0:T(8,128)(2,1)S(1)}, u32[]{:S(2)}, u32[]{:S(2)}) async-start(bf16[32,8,1024]{2,1,0:T(8,128)(2,1)} %get-tuple-element.52), calls=%async_computation | async-start | bytes 1048576 | tf_op jit(solution)/shard_map/all_to_all | solution.py:511
  25.3 1.6 collective-permute-start.4
  26.9 1.5 collective-permute-start.2
  28.8 1.2 collective-permute-start.3
  30.0 11.1 %student.1 = (bf16[8,1024,256]{2,1,0:T(8,128)(2,1)}, f32[4,128]{1,0:T(4,128)}, f32[512,256]{1,0:T(8,128)}) custom-call(bf16[512,256]{1,0:T(8,128)(2,1)} %feat.5, bf16[8,1024,256]{2,1,0:T(8,128)(2,1)} %bitcast.23), custom_call_target="tpu_custom_call" | custom-call | flops 4294967296 | bytes 8388608 | tf_op jit(solution)/shard_map/student/pallas_call | solution.py:173
  41.7 2.9 %collective-permute-done.2.refs_4_ = bf16[256,512]{1,0:T(8,128)(2,1)S(1)} collective-permute-done((bf16[256,512]{1,0:T(8,128)(2,1)S(1)}, bf16[256,512]{1,0:T(8,128)(2,1)S(1)}, u32[]{:S(2)}, u32[]{:S(2)}) %collective-permute-start.2) | collective-permute-done | bytes 262176 | tf_op jit(solution)/shard_map/ppermute | solution.py:520
  44.7 1.8 collective-permute-start.10
  46.5 1.2 collective-permute-start.6
  48.6 3.4 %copy-done = bf16[8,512,1024]{2,1,0:T(8,128)(2,1)S(1)} copy-done((bf16[8,512,1024]{2,1,0:T(8,128)(2,1)S(1)}, bf16[8,512,1024]{2,1,0:T(8,128)(2,1)}, u32[]{:S(2)}) %copy-start) | copy-done | bytes 8388632
  52.6 2.6 %row_pass.2 = f32[8,8,128]{2,1,0:T(8,128)} custom-call(bf16[8,512,1024]{2,1,0:T(8,128)(2,1)S(1)} %copy-done, bf16[32,8,1024]{2,1,0:T(8,128)(2,1)S(1)} %all-to-all-done.got, f32[4,128]{1,0:T(4,128)S(1)} %copy-done.5), custom_call_target="tpu_custom_call" | custom-call | flops 8388608 | bytes 65536 | tf_op jit(solution)/shard_map/row_pass/pallas_call | solution.py:258
  55.3 4.6 %all-to-all-start.1 = ((f32[8,8,128]{2,1,0:T(8,128)}), f32[8,8,128]{2,1,0:T(8,128)S(1)}, u32[]{:S(2)}, u32[]{:S(2)}) async-start(f32[8,8,128]{2,1,0:T(8,128)} %row_pass.2), calls=%async_computation.1 | async-start | bytes 65536 | tf_op jit(solution)/shard_map/all_to_all | solution.py:511
  59.9 4.7 %all-to-all-done.1.got = f32[8,8,128]{2,1,0:T(8,128)S(1)} async-done(((f32[8,8,128]{2,1,0:T(8,128)}), f32[8,8,128]{2,1,0:T(8,128)S(1)}, u32[]{:S(2)}, u32[]{:S(2)}) %all-to-all-start.1) | async-done | bytes 32800 | tf_op jit(solution)/shard_map/all_to_all | solution.py:511
  64.7 3.6 %copy-done.1 = bf16[8,512,1024]{2,1,0:T(8,128)(2,1)S(1)} copy-done((bf16[8,512,1024]{2,1,0:T(8,128)(2,1)S(1)}, bf16[8,512,1024]{2,1,0:T(8,128)(2,1)}, u32[]{:S(2)}) %copy-start.1) | copy-done | bytes 8388632
  68.3 1.9 col_pass.2
  70.3 2.8 %collective-permute-start.11 = (bf16[8,1024]{1,0:T(8,128)(2,1)S(1)}, bf16[8,1024]{1,0:T(8,128)(2,1)S(1)}, u32[]{:S(2)}, u32[]{:S(2)}) collective-permute-start(bf16[8,1024]{1,0:T(8,128)(2,1)S(1)} %bitcast.17), channel_id=1, source_target_pairs={{0,128},{64,192},{128,0},{192,64},{1,129},{65,193},{129,1},{193,65... | collective-permute-start | bytes 49160 | tf_op jit(solution)/shard_map/ppermute | solution.py:520
  73.4 2.3 %collective-permute-start.13 = (bf16[8,1024]{1,0:T(8,128)(2,1)S(1)}, bf16[8,1024]{1,0:T(8,128)(2,1)S(1)}, u32[]{:S(2)}, u32[]{:S(2)}) collective-permute-start(bf16[8,1024]{1,0:T(8,128)(2,1)S(1)} %bitcast.19), channel_id=1, source_target_pairs={{0,192},{64,0},{128,64},{192,128},{1,193},{65,1},{129,65},{193,129... | collective-permute-start | bytes 49160 | tf_op jit(solution)/shard_map/ppermute | solution.py:520
  75.8 1.1 collective-permute-done.12
  77.6 5.3 %all-to-all-start.2 = ((bf16[8,8,1152]{2,1,0:T(8,128)(2,1)}), bf16[8,8,1152]{2,1,0:T(8,128)(2,1)S(1)}, u32[]{:S(2)}, u32[]{:S(2)}) async-start(bf16[8,8,1152]{2,1,0:T(8,128)(2,1)} %broadcast_in_dim.2), calls=%async_computation.2 | async-start | bytes 294912 | tf_op jit(solution)/shard_map/all_to_all | solution.py:511
  82.9 1.5 collective-permute-start.14
  84.4 3.0 %collective-permute-start.15 = (bf16[256,512]{1,0:T(8,128)(2,1)S(1)}, bf16[256,512]{1,0:T(8,128)(2,1)S(1)}, u32[]{:S(2)}, u32[]{:S(2)}) collective-permute-start(bf16[256,512]{1,0:T(8,128)(2,1)S(1)} %collective-permute-done.5.refs_6_), channel_id=1, source_target_pairs={{0,1},{1,0},{2,3},{3,2},{4,5},{5,4},{6,7},{7,6},{8,9},{9,8},{10,11... | collective-permute-start | bytes 786440 | tf_op jit(solution)/shard_map/ppermute | solution.py:515
  87.5 3.7 %all-to-all-done.2.got.refs_19_ = bf16[8,8,1152]{2,1,0:T(8,128)(2,1)S(1)} async-done(((bf16[8,8,1152]{2,1,0:T(8,128)(2,1)}), bf16[8,8,1152]{2,1,0:T(8,128)(2,1)S(1)}, u32[]{:S(2)}, u32[]{:S(2)}) %all-to-all-start.2) | async-done | bytes 147488 | tf_op jit(solution)/shard_map/all_to_all | solution.py:511
  91.2 3.4 %copy-done.2 = bf16[8,512,1024]{2,1,0:T(8,128)(2,1)S(1)} copy-done((bf16[8,512,1024]{2,1,0:T(8,128)(2,1)S(1)}, bf16[8,512,1024]{2,1,0:T(8,128)(2,1)}, u32[]{:S(2)}) %copy-start.2) | copy-done | bytes 8388632
  94.5 2.7 %row_pass.3 = f32[8,8,128]{2,1,0:T(8,128)} custom-call(bf16[8,512,1024]{2,1,0:T(8,128)(2,1)S(1)} %copy-done.2, bf16[8,8,1152]{2,1,0:T(8,128)(2,1)S(1)} %all-to-all-done.2.got.refs_19_, f32[4,128]{1,0:T(4,128)S(1)} %copy-done.6), custom_call_target="tpu_custom_call" | custom-call | flops 8388608 | bytes 65536 | tf_op jit(solution)/shard_map/row_pass/pallas_call | solution.py:258
  97.2 7.6 %all-to-all-start.3 = ((f32[8,8,128]{2,1,0:T(8,128)}), f32[8,8,128]{2,1,0:T(8,128)S(1)}, u32[]{:S(2)}, u32[]{:S(2)}) async-start(f32[8,8,128]{2,1,0:T(8,128)} %row_pass.3), calls=%async_computation.3 | async-start | bytes 65536 | tf_op jit(solution)/shard_map/all_to_all | solution.py:511
  104.9 4.7 %all-to-all-done.3.got = f32[8,8,128]{2,1,0:T(8,128)S(1)} async-done(((f32[8,8,128]{2,1,0:T(8,128)}), f32[8,8,128]{2,1,0:T(8,128)S(1)}, u32[]{:S(2)}, u32[]{:S(2)}) %all-to-all-start.3) | async-done | bytes 32800 | tf_op jit(solution)/shard_map/all_to_all | solution.py:511
  110.3 3.4 %copy-done.3 = bf16[8,512,1024]{2,1,0:T(8,128)(2,1)S(1)} copy-done((bf16[8,512,1024]{2,1,0:T(8,128)(2,1)S(1)}, bf16[8,512,1024]{2,1,0:T(8,128)(2,1)}, u32[]{:S(2)}) %copy-start.3) | copy-done | bytes 8388632
  113.7 2.8 %col_pass.3 = (bf16[32,8,1024]{2,1,0:T(8,128)(2,1)}, bf16[8,128]{1,0:T(8,128)(2,1)}) custom-call(bf16[8,512,1024]{2,1,0:T(8,128)(2,1)S(1)} %copy-done.3, f32[8,8,128]{2,1,0:T(8,128)S(1)} %all-to-all-done.3.got), custom_call_target="tpu_custom_call" | custom-call | flops 8388608 | bytes 1048576 | tf_op jit(solution)/shard_map/col_pass/pallas_call | solution.py:293
  116.5 4.7 %all-to-all-start.4 = ((bf16[32,8,1024]{2,1,0:T(8,128)(2,1)}), bf16[32,8,1024]{2,1,0:T(8,128)(2,1)S(1)}, u32[]{:S(2)}, u32[]{:S(2)}) async-start(bf16[32,8,1024]{2,1,0:T(8,128)(2,1)} %get-tuple-element.78), calls=%async_computation.4 | async-start | bytes 1048576 | tf_op jit(solution)/shard_map/all_to_all | solution.py:511
  121.8 13.1 %early.1 = (bf16[8,512,512]{2,1,0:T(8,128)(2,1)}, bf16[1024,256]{1,0:T(8,128)(2,1)}, f32[1024,256]{1,0:T(8,128)}) custom-call(s32[11]{0:T(128)} %pad_add_fusion.refs_0_.pos, bf16[256,512]{1,0:T(8,128)(2,1)} %copy-done.9, bf16[256,512]{1,0:T(8,128)(2,1)} %copy-done.12, bf16[256,512]{1,0:T(8,128)(2,1)} %copy-done.13, bf16[256,512]{1,0:T(8,128)(2,1)} %copy-done.15, ...), custom_call_target="tpu_custom_call" | custom-call | flops 4294967296 | bytes 4194304 | tf_op jit(solution)/shard_map/early/pallas_call | solution.py:389
  134.9 1.1 all-to-all-done.4.got
  136.8 5.9 %row_last.1 = (f32[64,4,128]{2,1,0:T(4,128)}, f32[8,1024]{1,0:T(8,128)}) custom-call(bf16[8,512,1024]{2,1,0:T(8,128)(2,1)} %get-tuple-element.56.expo, bf16[32,8,1024]{2,1,0:T(8,128)(2,1)} %copy-done.7), custom_call_target="tpu_custom_call" | custom-call | flops 8388608 | bytes 8388608 | tf_op jit(solution)/shard_map/row_last/pallas_call | solution.py:225
  142.7 8.5 %all-to-all-start.5 = ((f32[64,4,128]{2,1,0:T(4,128)}), f32[64,4,128]{2,1,0:T(4,128)S(1)}, u32[]{:S(2)}, u32[]{:S(2)}) async-start(f32[64,4,128]{2,1,0:T(4,128)} %get-tuple-element.81), calls=%async_computation.5 | async-start | bytes 262144 | tf_op jit(solution)/shard_map/all_to_all | solution.py:511
  151.2 8.2 %mix_pass.1 = (f32[512,256]{1,0:T(8,128)}, f32[1,512]{1,0:T(1,128)}) custom-call(bf16[8,512,1024]{2,1,0:T(8,128)(2,1)} %get-tuple-element.56.expo, f32[8,1024]{1,0:T(8,128)} %get-tuple-element.82.col, bf16[8,1024,256]{2,1,0:T(8,128)(2,1)} %get-tuple-element.75.dirs, bf16[512,256]{1,0:T(8,128)(2,1)} %feat.5), custom_call_target="tpu_custom_call" | custom-call | flops 2147483648 | bytes 12582912 | tf_op jit(solution)/shard_map/mix_pass/pallas_call | solution.py:331
  159.4 2.9 %all-to-all-done.5 = f32[64,4,128]{2,1,0:T(4,128)S(1)} async-done(((f32[64,4,128]{2,1,0:T(4,128)}), f32[64,4,128]{2,1,0:T(4,128)S(1)}, u32[]{:S(2)}, u32[]{:S(2)}) %all-to-all-start.5) | async-done | bytes 131104 | tf_op jit(solution)/shard_map/all_to_all | solution.py:511
  163.0 11.7 %proto_part.1 = (f32[256,256]{1,0:T(8,128)}, bf16[3,256,256]{2,1,0:T(8,128)(2,1)}, f32[264,256]{1,0:T(8,128)}, bf16[272,256]{1,0:T(8,128)(2,1)}, f32[1,512]{1,0:T(1,128)}) custom-call(s32[11]{0:T(128)} %pad_add_fusion.refs_0_.pos, bf16[1024,256]{1,0:T(8,128)(2,1)} %get-tuple-element.76.dirs, bf16[8,512,512]{2,1,0:T(8,128)(2,1)} %get-tuple-element.77.rows, ...), custom_call_target="tpu_custom_call" | custom-call | flops 4294967296 | bytes 4194304 | tf_op jit(solution)/shard_map/proto_part/pallas_call | solution.py:481
  175.2 1.1 collective-permute-done.18
  176.4 1.0 fusion.2
  178.2 1.3 collective-permute-start.19
  179.5 2.7 %collective-permute-start.21 = (bf16[272,256]{1,0:T(8,128)(2,1)S(1)}, bf16[272,256]{1,0:T(8,128)(2,1)S(1)}, u32[]{:S(2)}, u32[]{:S(2)}) collective-permute-start(bf16[272,256]{1,0:T(8,128)(2,1)S(1)} %get-tuple-element.109), channel_id=1, source_target_pairs={{0,6},{2,0},{4,2},{6,4},{1,7},{3,1},{5,3},{7,5},{8,14},{10,8},{12,... | collective-permute-start | bytes 417800 | tf_op jit(solution)/shard_map/ppermute | solution.py:520
  182.2 1.1 slice_bitcast_fusion.2
  183.7 2.2 %collective-permute-start.24 = (bf16[256,256]{1,0:T(8,128)(2,1)S(1)}, bf16[256,256]{1,0:T(8,128)(2,1)S(1)}, u32[]{:S(2)}, u32[]{:S(2)}) collective-permute-start(bf16[256,256]{1,0:T(8,128)(2,1)S(1)} %get-tuple-element.105), channel_id=1, source_target_pairs={{0,128},{64,192},{128,0},{192,64},{1,129},{65,193},{129,1},{193,65... | collective-permute-start | bytes 393224 | tf_op jit(solution)/shard_map/ppermute | solution.py:520
  185.9 1.1 collective-permute-start.25
  187.0 1.4 collective-permute-done.20
  189.4 1.2 collective-permute-done.24
  (112 shorter events, 12.4 us)
Async XLA Ops:
  1.7 23.7 %copy-start.9 = (bf16[256,512]{1,0:T(8,128)(2,1)}, bf16[256,512]{1,0:T(8,128)(2,1)S(1)}, u32[]{:S(2)}) copy-start(bf16[256,512]{1,0:T(8,128)(2,1)S(1)} %pad_maximum_fusion.refs_1_) | copy-start | bytes 786436
  1.7 15.6 %collective-permute-start = (bf16[256,512]{1,0:T(8,128)(2,1)S(1)}, bf16[256,512]{1,0:T(8,128)(2,1)S(1)}, u32[]{:S(2)}, u32[]{:S(2)}) collective-permute-start(bf16[256,512]{1,0:T(8,128)(2,1)S(1)} %pad_maximum_fusion.refs_1_), channel_id=1, source_target_pairs={{0,8},{8,16},{16,24},{24,32},{32,40},{40,48},{48,56},{56,0},{1,9},... | collective-permute-start | bytes 786440 | tf_op jit(solution)/shard_map/ppermute | solution.py:520
  4.2 13.0 %collective-permute-start.1 = (bf16[256,512]{1,0:T(8,128)(2,1)S(1)}, bf16[256,512]{1,0:T(8,128)(2,1)S(1)}, u32[]{:S(2)}, u32[]{:S(2)}) collective-permute-start(bf16[256,512]{1,0:T(8,128)(2,1)S(1)} %pad_maximum_fusion.refs_1_), channel_id=1, source_target_pairs={{0,56},{8,0},{16,8},{24,16},{32,24},{40,32},{48,40},{56,48},{1,57}... | collective-permute-start | bytes 786440 | tf_op jit(solution)/shard_map/ppermute | solution.py:520
  17.2 23.9 %copy-start.12 = (bf16[256,512]{1,0:T(8,128)(2,1)}, bf16[256,512]{1,0:T(8,128)(2,1)S(1)}, u32[]{:S(2)}) copy-start(bf16[256,512]{1,0:T(8,128)(2,1)S(1)} %collective-permute-done.refs_2_) | copy-start | bytes 786436
  17.2 23.9 %copy-start.13 = (bf16[256,512]{1,0:T(8,128)(2,1)}, bf16[256,512]{1,0:T(8,128)(2,1)S(1)}, u32[]{:S(2)}) copy-start(bf16[256,512]{1,0:T(8,128)(2,1)S(1)} %collective-permute-done.1.refs_3_) | copy-start | bytes 786436
  17.3 27.4 %all-to-all-start = ((bf16[32,8,1024]{2,1,0:T(8,128)(2,1)}), bf16[32,8,1024]{2,1,0:T(8,128)(2,1)S(1)}, u32[]{:S(2)}, u32[]{:S(2)}) async-start(bf16[32,8,1024]{2,1,0:T(8,128)(2,1)} %get-tuple-element.52), calls=%async_computation | async-start | bytes 1048576 | tf_op jit(solution)/shard_map/all_to_all | solution.py:511
  25.3 16.4 %collective-permute-start.4 = (bf16[256,512]{1,0:T(8,128)(2,1)S(1)}, bf16[256,512]{1,0:T(8,128)(2,1)S(1)}, u32[]{:S(2)}, u32[]{:S(2)}) collective-permute-start(bf16[256,512]{1,0:T(8,128)(2,1)S(1)} %pad_maximum_fusion.refs_1_), channel_id=1, source_target_pairs={{0,1},{1,0},{2,3},{3,2},{4,5},{5,4},{6,7},{7,6},{8,9},{9,8},{10,11... | collective-permute-start | bytes 786440 | tf_op jit(solution)/shard_map/ppermute | solution.py:515
  26.9 17.7 %collective-permute-start.2 = (bf16[256,512]{1,0:T(8,128)(2,1)S(1)}, bf16[256,512]{1,0:T(8,128)(2,1)S(1)}, u32[]{:S(2)}, u32[]{:S(2)}) collective-permute-start(bf16[256,512]{1,0:T(8,128)(2,1)S(1)} %collective-permute-done.refs_2_), channel_id=1, source_target_pairs={{0,8},{8,16},{16,24},{24,32},{32,40},{40,48},{48,56},{56,0},{1,9},... | collective-permute-start | bytes 786440 | tf_op jit(solution)/shard_map/ppermute | solution.py:520
  28.5 19.5 %collective-permute-start.7 = (bf16[256,512]{1,0:T(8,128)(2,1)S(1)}, bf16[256,512]{1,0:T(8,128)(2,1)S(1)}, u32[]{:S(2)}, u32[]{:S(2)}) collective-permute-start(bf16[256,512]{1,0:T(8,128)(2,1)S(1)} %collective-permute-done.refs_2_), channel_id=1, source_target_pairs={{0,1},{1,0},{2,3},{3,2},{4,5},{5,4},{6,7},{7,6},{8,9},{9,8},{10,11... | collective-permute-start | bytes 786440 | tf_op jit(solution)/shard_map/ppermute | solution.py:515
  28.8 15.8 %collective-permute-start.3 = (bf16[256,512]{1,0:T(8,128)(2,1)S(1)}, bf16[256,512]{1,0:T(8,128)(2,1)S(1)}, u32[]{:S(2)}, u32[]{:S(2)}) collective-permute-start(bf16[256,512]{1,0:T(8,128)(2,1)S(1)} %collective-permute-done.1.refs_3_), channel_id=1, source_target_pairs={{0,56},{8,0},{16,8},{24,16},{32,24},{40,32},{48,40},{56,48},{1,57}... | collective-permute-start | bytes 786440 | tf_op jit(solution)/shard_map/ppermute | solution.py:520
  41.1 18.8 %collective-permute-start.8 = (bf16[256,512]{1,0:T(8,128)(2,1)S(1)}, bf16[256,512]{1,0:T(8,128)(2,1)S(1)}, u32[]{:S(2)}, u32[]{:S(2)}) collective-permute-start(bf16[256,512]{1,0:T(8,128)(2,1)S(1)} %collective-permute-done.1.refs_3_), channel_id=1, source_target_pairs={{0,1},{1,0},{2,3},{3,2},{4,5},{5,4},{6,7},{7,6},{8,9},{9,8},{10,11... | collective-permute-start | bytes 786440 | tf_op jit(solution)/shard_map/ppermute | solution.py:515
  41.7 13.6 %copy-start.14 = (bf16[256,512]{1,0:T(8,128)(2,1)}, bf16[256,512]{1,0:T(8,128)(2,1)S(1)}, u32[]{:S(2)}) copy-start(bf16[256,512]{1,0:T(8,128)(2,1)S(1)} %collective-permute-done.4.refs_9_) | copy-start | bytes 786436
  44.6 10.6 %copy-start.15 = (bf16[256,512]{1,0:T(8,128)(2,1)}, bf16[256,512]{1,0:T(8,128)(2,1)S(1)}, u32[]{:S(2)}) copy-start(bf16[256,512]{1,0:T(8,128)(2,1)S(1)} %collective-permute-done.2.refs_4_) | copy-start | bytes 786436
  44.7 10.6 %copy-start.17 = (bf16[256,512]{1,0:T(8,128)(2,1)}, bf16[256,512]{1,0:T(8,128)(2,1)S(1)}, u32[]{:S(2)}) copy-start(bf16[256,512]{1,0:T(8,128)(2,1)S(1)} %collective-permute-done.3.refs_5_) | copy-start | bytes 786436
  44.7 20.0 %collective-permute-start.10 = (bf16[256,512]{1,0:T(8,128)(2,1)S(1)}, bf16[256,512]{1,0:T(8,128)(2,1)S(1)}, u32[]{:S(2)}, u32[]{:S(2)}) collective-permute-start(bf16[256,512]{1,0:T(8,128)(2,1)S(1)} %collective-permute-done.3.refs_5_), channel_id=1, source_target_pairs={{0,1},{1,0},{2,3},{3,2},{4,5},{5,4},{6,7},{7,6},{8,9},{9,8},{10,11... | collective-permute-start | bytes 786440 | tf_op jit(solution)/shard_map/ppermute | solution.py:515
  46.5 18.2 %collective-permute-start.6 = (bf16[256,512]{1,0:T(8,128)(2,1)S(1)}, bf16[256,512]{1,0:T(8,128)(2,1)S(1)}, u32[]{:S(2)}, u32[]{:S(2)}) collective-permute-start(bf16[256,512]{1,0:T(8,128)(2,1)S(1)} %collective-permute-done.3.refs_5_), channel_id=1, source_target_pairs={{0,56},{8,0},{16,8},{24,16},{32,24},{40,32},{48,40},{56,48},{1,57}... | collective-permute-start | bytes 786440 | tf_op jit(solution)/shard_map/ppermute | solution.py:520
  47.7 17.0 %collective-permute-start.5 = (bf16[256,512]{1,0:T(8,128)(2,1)S(1)}, bf16[256,512]{1,0:T(8,128)(2,1)S(1)}, u32[]{:S(2)}, u32[]{:S(2)}) collective-permute-start(bf16[256,512]{1,0:T(8,128)(2,1)S(1)} %collective-permute-done.2.refs_4_), channel_id=1, source_target_pairs={{0,8},{8,16},{16,24},{24,32},{32,40},{40,48},{48,56},{56,0},{1,9},... | collective-permute-start | bytes 786440 | tf_op jit(solution)/shard_map/ppermute | solution.py:520
  47.9 16.7 %collective-permute-start.9 = (bf16[256,512]{1,0:T(8,128)(2,1)S(1)}, bf16[256,512]{1,0:T(8,128)(2,1)S(1)}, u32[]{:S(2)}, u32[]{:S(2)}) collective-permute-start(bf16[256,512]{1,0:T(8,128)(2,1)S(1)} %collective-permute-done.2.refs_4_), channel_id=1, source_target_pairs={{0,1},{1,0},{2,3},{3,2},{4,5},{5,4},{6,7},{7,6},{8,9},{9,8},{10,11... | collective-permute-start | bytes 786440 | tf_op jit(solution)/shard_map/ppermute | solution.py:515
  55.3 35.9 %copy-start.6 = (f32[4,128]{1,0:T(4,128)S(1)}, f32[4,128]{1,0:T(4,128)}, u32[]{:S(2)}) copy-start(f32[4,128]{1,0:T(4,128)} %get-tuple-element.58.tot) | copy-start | bytes 6148
  55.3 9.3 %all-to-all-start.1 = ((f32[8,8,128]{2,1,0:T(8,128)}), f32[8,8,128]{2,1,0:T(8,128)S(1)}, u32[]{:S(2)}, u32[]{:S(2)}) async-start(f32[8,8,128]{2,1,0:T(8,128)} %row_pass.2), calls=%async_computation.1 | async-start | bytes 65536 | tf_op jit(solution)/shard_map/all_to_all | solution.py:511
  59.9 10.3 %copy-start.18 = (bf16[256,512]{1,0:T(8,128)(2,1)}, bf16[256,512]{1,0:T(8,128)(2,1)S(1)}, u32[]{:S(2)}) copy-start(bf16[256,512]{1,0:T(8,128)(2,1)S(1)} %collective-permute-done.8.refs_11_) | copy-start | bytes 786436
  64.7 19.7 %copy-start.21 = (bf16[256,512]{1,0:T(8,128)(2,1)}, bf16[256,512]{1,0:T(8,128)(2,1)S(1)}, u32[]{:S(2)}) copy-start(bf16[256,512]{1,0:T(8,128)(2,1)S(1)} %collective-permute-done.5.refs_6_) | copy-start | bytes 786436
  64.7 22.7 %copy-start.20 = (bf16[256,512]{1,0:T(8,128)(2,1)}, bf16[256,512]{1,0:T(8,128)(2,1)S(1)}, u32[]{:S(2)}) copy-start(bf16[256,512]{1,0:T(8,128)(2,1)S(1)} %collective-permute-done.6.refs_7_) | copy-start | bytes 786436
  70.3 5.5 %collective-permute-start.11 = (bf16[8,1024]{1,0:T(8,128)(2,1)S(1)}, bf16[8,1024]{1,0:T(8,128)(2,1)S(1)}, u32[]{:S(2)}, u32[]{:S(2)}) collective-permute-start(bf16[8,1024]{1,0:T(8,128)(2,1)S(1)} %bitcast.17), channel_id=1, source_target_pairs={{0,128},{64,192},{128,0},{192,64},{1,129},{65,193},{129,1},{193,65... | collective-permute-start | bytes 49160 | tf_op jit(solution)/shard_map/ppermute | solution.py:520
  73.1 3.8 %collective-permute-start.12 = (bf16[8,1024]{1,0:T(8,128)(2,1)S(1)}, bf16[8,1024]{1,0:T(8,128)(2,1)S(1)}, u32[]{:S(2)}, u32[]{:S(2)}) collective-permute-start(bf16[8,1024]{1,0:T(8,128)(2,1)S(1)} %bitcast.18), channel_id=1, source_target_pairs={{0,64},{64,128},{128,192},{192,0},{1,65},{65,129},{129,193},{193,1... | collective-permute-start | bytes 49160 | tf_op jit(solution)/shard_map/ppermute | solution.py:520
  73.4 3.5 %collective-permute-start.13 = (bf16[8,1024]{1,0:T(8,128)(2,1)S(1)}, bf16[8,1024]{1,0:T(8,128)(2,1)S(1)}, u32[]{:S(2)}, u32[]{:S(2)}) collective-permute-start(bf16[8,1024]{1,0:T(8,128)(2,1)S(1)} %bitcast.19), channel_id=1, source_target_pairs={{0,192},{64,0},{128,64},{192,128},{1,193},{65,1},{129,65},{193,129... | collective-permute-start | bytes 49160 | tf_op jit(solution)/shard_map/ppermute | solution.py:520
  77.6 13.6 %all-to-all-start.2 = ((bf16[8,8,1152]{2,1,0:T(8,128)(2,1)}), bf16[8,8,1152]{2,1,0:T(8,128)(2,1)S(1)}, u32[]{:S(2)}, u32[]{:S(2)}) async-start(bf16[8,8,1152]{2,1,0:T(8,128)(2,1)} %broadcast_in_dim.2), calls=%async_computation.2 | async-start | bytes 294912 | tf_op jit(solution)/shard_map/all_to_all | solution.py:511
  82.9 21.9 %collective-permute-start.14 = (bf16[256,512]{1,0:T(8,128)(2,1)S(1)}, bf16[256,512]{1,0:T(8,128)(2,1)S(1)}, u32[]{:S(2)}, u32[]{:S(2)}) collective-permute-start(bf16[256,512]{1,0:T(8,128)(2,1)S(1)} %collective-permute-done.5.refs_6_), channel_id=1, source_target_pairs={{0,8},{8,16},{16,24},{24,32},{32,40},{40,48},{48,56},{56,0},{1,9},... | collective-permute-start | bytes 786440 | tf_op jit(solution)/shard_map/ppermute | solution.py:520
  84.4 20.4 %collective-permute-start.15 = (bf16[256,512]{1,0:T(8,128)(2,1)S(1)}, bf16[256,512]{1,0:T(8,128)(2,1)S(1)}, u32[]{:S(2)}, u32[]{:S(2)}) collective-permute-start(bf16[256,512]{1,0:T(8,128)(2,1)S(1)} %collective-permute-done.5.refs_6_), channel_id=1, source_target_pairs={{0,1},{1,0},{2,3},{3,2},{4,5},{5,4},{6,7},{7,6},{8,9},{9,8},{10,11... | collective-permute-start | bytes 786440 | tf_op jit(solution)/shard_map/ppermute | solution.py:515
  87.4 17.5 %collective-permute-start.16 = (bf16[256,512]{1,0:T(8,128)(2,1)S(1)}, bf16[256,512]{1,0:T(8,128)(2,1)S(1)}, u32[]{:S(2)}, u32[]{:S(2)}) collective-permute-start(bf16[256,512]{1,0:T(8,128)(2,1)S(1)} %collective-permute-done.6.refs_7_), channel_id=1, source_target_pairs={{0,1},{1,0},{2,3},{3,2},{4,5},{5,4},{6,7},{7,6},{8,9},{9,8},{10,11... | collective-permute-start | bytes 786440 | tf_op jit(solution)/shard_map/ppermute | solution.py:515
  97.2 23.9 %copy-start.27 = (s32[8]{0:T(128)S(1)}, s32[8]{0:T(128)}, u32[]{:S(2)}) copy-start(s32[8]{0:T(128)} %constant.39.clone) | copy-start | bytes 100
  97.2 12.3 %all-to-all-start.3 = ((f32[8,8,128]{2,1,0:T(8,128)}), f32[8,8,128]{2,1,0:T(8,128)S(1)}, u32[]{:S(2)}, u32[]{:S(2)}) async-start(f32[8,8,128]{2,1,0:T(8,128)} %row_pass.3), calls=%async_computation.3 | async-start | bytes 65536 | tf_op jit(solution)/shard_map/all_to_all | solution.py:511
  104.8 11.6 %copy-start.23 = (bf16[256,512]{1,0:T(8,128)(2,1)}, bf16[256,512]{1,0:T(8,128)(2,1)S(1)}, u32[]{:S(2)}) copy-start(bf16[256,512]{1,0:T(8,128)(2,1)S(1)} %collective-permute-done.14.refs_8_) | copy-start | bytes 786436
  104.8 11.6 %copy-start.24 = (bf16[256,512]{1,0:T(8,128)(2,1)}, bf16[256,512]{1,0:T(8,128)(2,1)S(1)}, u32[]{:S(2)}) copy-start(bf16[256,512]{1,0:T(8,128)(2,1)S(1)} %collective-permute-done.15.refs_14_) | copy-start | bytes 786436
  104.9 11.6 %copy-start.25 = (bf16[256,512]{1,0:T(8,128)(2,1)}, bf16[256,512]{1,0:T(8,128)(2,1)S(1)}, u32[]{:S(2)}) copy-start(bf16[256,512]{1,0:T(8,128)(2,1)S(1)} %collective-permute-done.16.refs_15_) | copy-start | bytes 786436
  109.6 6.9 %collective-permute-start.17 = (bf16[256,512]{1,0:T(8,128)(2,1)S(1)}, bf16[256,512]{1,0:T(8,128)(2,1)S(1)}, u32[]{:S(2)}, u32[]{:S(2)}) collective-permute-start(bf16[256,512]{1,0:T(8,128)(2,1)S(1)} %collective-permute-done.14.refs_8_), channel_id=1, source_target_pairs={{0,1},{1,0},{2,3},{3,2},{4,5},{5,4},{6,7},{7,6},{8,9},{9,8},{10,11... | collective-permute-start | bytes 786440 | tf_op jit(solution)/shard_map/ppermute | solution.py:515
  116.5 19.5 %all-to-all-start.4 = ((bf16[32,8,1024]{2,1,0:T(8,128)(2,1)}), bf16[32,8,1024]{2,1,0:T(8,128)(2,1)S(1)}, u32[]{:S(2)}, u32[]{:S(2)}) async-start(bf16[32,8,1024]{2,1,0:T(8,128)(2,1)} %get-tuple-element.78), calls=%async_computation.4 | async-start | bytes 1048576 | tf_op jit(solution)/shard_map/all_to_all | solution.py:511
  142.7 19.6 %all-to-all-start.5 = ((f32[64,4,128]{2,1,0:T(4,128)}), f32[64,4,128]{2,1,0:T(4,128)S(1)}, u32[]{:S(2)}, u32[]{:S(2)}) async-start(f32[64,4,128]{2,1,0:T(4,128)} %get-tuple-element.81), calls=%async_computation.5 | async-start | bytes 262144 | tf_op jit(solution)/shard_map/all_to_all | solution.py:511
  174.7 16.8 %copy-start.8 = (f32[256,256]{1,0:T(8,128)S(1)}, f32[256,256]{1,0:T(8,128)}, u32[]{:S(2)}) copy-start(f32[256,256]{1,0:T(8,128)} %get-tuple-element.93) | copy-start | bytes 786436
  174.7 18.4 %copy-start.11 = (f32[1,512]{1,0:T(1,128)S(1)}, f32[1,512]{1,0:T(1,128)}, u32[]{:S(2)}) copy-start(f32[1,512]{1,0:T(1,128)} %get-tuple-element.90) | copy-start | bytes 6148
  174.7 1.7 collective-permute-start.18
  178.2 7.6 %collective-permute-start.19 = (bf16[272,256]{1,0:T(8,128)(2,1)S(1)}, bf16[272,256]{1,0:T(8,128)(2,1)S(1)}, u32[]{:S(2)}, u32[]{:S(2)}) collective-permute-start(bf16[272,256]{1,0:T(8,128)(2,1)S(1)} %get-tuple-element.109), channel_id=1, source_target_pairs={{0,4},{2,6},{4,0},{6,2},{1,5},{3,7},{5,1},{7,3},{8,12},{10,14},{12... | collective-permute-start | bytes 417800 | tf_op jit(solution)/shard_map/ppermute | solution.py:520
  179.5 8.9 %collective-permute-start.20 = (bf16[272,256]{1,0:T(8,128)(2,1)S(1)}, bf16[272,256]{1,0:T(8,128)(2,1)S(1)}, u32[]{:S(2)}, u32[]{:S(2)}) collective-permute-start(bf16[272,256]{1,0:T(8,128)(2,1)S(1)} %get-tuple-element.109), channel_id=1, source_target_pairs={{0,2},{2,4},{4,6},{6,0},{1,3},{3,5},{5,7},{7,1},{8,10},{10,12},{12... | collective-permute-start | bytes 417800 | tf_op jit(solution)/shard_map/ppermute | solution.py:520
  179.5 8.9 %collective-permute-start.21 = (bf16[272,256]{1,0:T(8,128)(2,1)S(1)}, bf16[272,256]{1,0:T(8,128)(2,1)S(1)}, u32[]{:S(2)}, u32[]{:S(2)}) collective-permute-start(bf16[272,256]{1,0:T(8,128)(2,1)S(1)} %get-tuple-element.109), channel_id=1, source_target_pairs={{0,6},{2,0},{4,2},{6,4},{1,7},{3,1},{5,3},{7,5},{8,14},{10,8},{12,... | collective-permute-start | bytes 417800 | tf_op jit(solution)/shard_map/ppermute | solution.py:520
  183.3 6.2 %collective-permute-start.23 = (bf16[256,256]{1,0:T(8,128)(2,1)S(1)}, bf16[256,256]{1,0:T(8,128)(2,1)S(1)}, u32[]{:S(2)}, u32[]{:S(2)}) collective-permute-start(bf16[256,256]{1,0:T(8,128)(2,1)S(1)} %get-tuple-element.103), channel_id=1, source_target_pairs={{0,64},{64,128},{128,192},{192,0},{1,65},{65,129},{129,193},{193,1... | collective-permute-start | bytes 393224 | tf_op jit(solution)/shard_map/ppermute | solution.py:520
  183.7 7.0 %collective-permute-start.24 = (bf16[256,256]{1,0:T(8,128)(2,1)S(1)}, bf16[256,256]{1,0:T(8,128)(2,1)S(1)}, u32[]{:S(2)}, u32[]{:S(2)}) collective-permute-start(bf16[256,256]{1,0:T(8,128)(2,1)S(1)} %get-tuple-element.105), channel_id=1, source_target_pairs={{0,128},{64,192},{128,0},{192,64},{1,129},{65,193},{129,1},{193,65... | collective-permute-start | bytes 393224 | tf_op jit(solution)/shard_map/ppermute | solution.py:520
  185.9 5.6 %collective-permute-start.25 = (bf16[256,256]{1,0:T(8,128)(2,1)S(1)}, bf16[256,256]{1,0:T(8,128)(2,1)S(1)}, u32[]{:S(2)}, u32[]{:S(2)}) collective-permute-start(bf16[256,256]{1,0:T(8,128)(2,1)S(1)} %get-tuple-element.104), channel_id=1, source_target_pairs={{0,192},{64,0},{128,64},{192,128},{1,193},{65,1},{129,65},{193,129... | collective-permute-start | bytes 393224 | tf_op jit(solution)/shard_map/ppermute | solution.py:520
  188.7 3.5 %collective-permute-start.22 = (bf16[272,256]{1,0:T(8,128)(2,1)S(1)}, bf16[272,256]{1,0:T(8,128)(2,1)S(1)}, u32[]{:S(2)}, u32[]{:S(2)}) collective-permute-start(bf16[272,256]{1,0:T(8,128)(2,1)S(1)} %maximum_maximum_fusion.1), channel_id=1, source_target_pairs={{0,1},{1,0},{2,3},{3,2},{4,5},{5,4},{6,7},{7,6},{8,9},{9,8},{10,11... | collective-permute-start | bytes 417800 | tf_op jit(solution)/shard_map/ppermute | solution.py:515
  (12 other events, 38.9 us)
